TPU v7x, 32 devices: a whole 2x2x4 slice. The times are simulated.
32 devices in a mesh: dp: 8 (over z, y), tensor: 4 (over x, core).
Axes of the slice: x: 2, y: 2, z: 4, core: 2. Of those that a mesh axis runs over, the one named last changes fastest.
Arguments:
- inputs: bfloat16 [12288, 768], P(('dp', 'tensor')), may hold values from -6 to 6
- segments: int32 [12288], P('dp'), may hold values from 0 to 8, as said below
- first_gain: bfloat16 [768], replicated, may hold values from 0.25 to 1.75
- query_weight: bfloat16 [768, 768], P(None, 'tensor'), may hold values from -0.078125 to 0.078125
- lookup_projection: bfloat16 [768, 768], P(None, 'tensor'), may hold values from -0.078125 to 0.078125
- value_weight: bfloat16 [768, 768], P(None, 'tensor'), may hold values from -0.21875 to 0.21875
- output_weight: bfloat16 [768, 768], P('tensor'), may hold values from -1.75 to 1.75
- bucket_bias_table: bfloat16 [32, 12], P(None, 'tensor'), may hold values from -4 to 4
- second_gain: bfloat16 [768], replicated, may hold values from 0.25 to 1.75
- inner_weight: bfloat16 [768, 3072], P(None, 'tensor'), may hold values from -0.21875 to 0.21875
- outer_weight: bfloat16 [3072, 768], P('tensor'), may hold values from -0.15625 to 0.15625
- cotangent: bfloat16 [12288, 768], P(('dp', 'tensor')), may hold values from -6 to 6
Outputs:
- layer_output: bfloat16 [12288, 768], P(('dp', 'tensor'))
- input_grad: float32 [12288, 768], P(('dp', 'tensor'))
- query_weight_grad: float32 [768, 768], P(None, 'tensor')
- key_weight_grad: float32 [768, 768], P(None, 'tensor')
- content_projection_adjoint: float32 [768, 768], P(None, 'tensor')
- output_weight_grad: float32 [768, 768], P('tensor')
- table_grad: float32 [32, 12], P(None, 'tensor')
- inner_weight_grad: float32 [768, 3072], P(None, 'tensor')
- outer_weight_grad: float32 [3072, 768], P('tensor')
- gain_grads: float32 [2, 768], replicated
Inputs may be any that keep to these rules, and one draw needn't show every extreme that they name: `segments`: each block of 1536 tokens holds whole sequences numbered 0, 1, 2, ... in order; the first has exactly 1024 tokens, the others are multiples of 64 tokens and at most 1024; in some block every sequence after the first has 64 tokens.
All inputs are finite; a program needn't handle non-finite values.
Results may differ from a plain program's by a relative error of at most 0.015.
Values may be sent and summed in bfloat16 or wider, within the bound.
No kernel may reach another device: no remote copies, remote signals or barrier semaphores. Data moves between devices by JAX's collectives and lax.ppermute only.
A program may use at most 128 MiB of HBM per device.

v0:
```python
import jax
import jax.numpy as jnp
from jax import lax
from jax.sharding import PartitionSpec as P

DH = 64


EDGES = (8, 12, 16, 23, 32, 46, 64, 91)
EPSILON = 1e-06
MASKED = -1000000000.0


def buckets_of(offset):
    distance = jnp.abs(offset)
    coarse = jnp.full(distance.shape, 7, jnp.int32)
    for boundary in EDGES:
        coarse = coarse + (distance >= boundary).astype(jnp.int32)
    bucket = jnp.where(distance < 8, distance, coarse)
    return bucket + jnp.where(offset > 0, 16, 0).astype(jnp.int32)


def root_norm(values, gains):
    inverse = lax.rsqrt(jnp.mean(values * values, axis=-1, keepdims=True) + EPSILON)
    return (values * inverse * gains, inverse)


def norm_input_grad(values, inverse, gains, upstream):
    scaled = upstream * gains
    projection = jnp.mean(scaled * values, axis=-1, keepdims=True)
    return inverse * scaled - values * (inverse * inverse * inverse) * projection


def norm_gain_grad(values, inverse, upstream):
    return jnp.sum(upstream * values * inverse, axis=0)


def smooth_gate(values):
    return jax.nn.gelu(values, approximate=True)


def bucket_onehot(bucket, count):
    slots = jnp.arange(count, dtype=jnp.int32)[:, None, None]
    return (bucket[None] == slots).astype(jnp.bfloat16)


def score_block(query_block, key_rows, row_start, segments, bucket_bias_table):
    row_count = query_block.shape[0]
    raw_scores = jnp.einsum(
        "qhd,khd->hqk", query_block, key_rows, preferred_element_type=jnp.float32
    )
    row_place = row_start + jnp.arange(row_count, dtype=jnp.int32)
    key_place = jnp.arange(key_rows.shape[0], dtype=jnp.int32)
    distance_class_onehot = bucket_onehot(
        buckets_of(key_place[None, :] - row_place[:, None]), bucket_bias_table.shape[0]
    )
    position_bias = jnp.einsum(
        "gmn,gi->imn", distance_class_onehot, bucket_bias_table, preferred_element_type=jnp.float32
    )
    row_segments = lax.dynamic_slice_in_dim(segments, row_start, row_count)
    visible_pairs_flag = row_segments[:, None] == segments[None, :]
    scores = jnp.where(visible_pairs_flag[None], raw_scores + position_bias, MASKED)
    return (scores, distance_class_onehot)


def attend_forward(queries, key_rows, value_rows, segments, bucket_bias_table, block_rows):
    total_rows = queries.shape[0]

    def step_forward(carried, block_number):
        row_start = block_number * block_rows
        query_block = lax.dynamic_slice_in_dim(queries, row_start, block_rows)
        scores, unused = score_block(query_block, key_rows, row_start, segments, bucket_bias_table)
        row_peak = jnp.max(scores, axis=-1, keepdims=True)
        weights = jnp.exp(scores - row_peak)
        row_total = jnp.sum(weights, axis=-1, keepdims=True)
        probability = (weights / row_total).astype(jnp.bfloat16)
        context = jnp.einsum(
            "hqk,khd->qhd", probability, value_rows, preferred_element_type=jnp.float32
        )
        return (carried, (context.astype(jnp.bfloat16), row_peak + jnp.log(row_total)))

    unused, (context, logsum) = lax.scan(
        step_forward, 0, jnp.arange(total_rows // block_rows, dtype=jnp.int32)
    )
    return (context.reshape(total_rows, -1), logsum)


def attend_backward(
    queries, key_rows, value_rows, segments, bucket_bias_table, logsum, context_grad, block_rows
):
    total_rows = queries.shape[0]

    def step_forward(carried, block_number):
        key_total, content_accumulated, table_total = carried
        row_start = block_number * block_rows
        query_block = lax.dynamic_slice_in_dim(queries, row_start, block_rows)
        grad_block = lax.dynamic_slice_in_dim(context_grad, row_start, block_rows)
        scores, distance_class_onehot = score_block(
            query_block, key_rows, row_start, segments, bucket_bias_table
        )
        probability = jnp.exp(scores - logsum[block_number])
        prob_grad = jnp.einsum(
            "qhd,khd->hqk", grad_block, value_rows, preferred_element_type=jnp.float32
        )
        row_dot = jnp.sum(probability * prob_grad, axis=-1, keepdims=True)
        logit_cotangent = (probability * (prob_grad - row_dot)).astype(jnp.bfloat16)
        query_part = jnp.einsum(
            "hqk,khd->qhd", logit_cotangent, key_rows, preferred_element_type=jnp.float32
        )
        key_total = key_total + jnp.einsum(
            "hqk,qhd->khd", logit_cotangent, query_block, preferred_element_type=jnp.float32
        )
        content_accumulated = content_accumulated + jnp.einsum(
            "hqk,qhd->khd",
            probability.astype(jnp.bfloat16),
            grad_block,
            preferred_element_type=jnp.float32,
        )
        table_part = jnp.einsum(
            "swf,kwf->ks",
            logit_cotangent,
            distance_class_onehot,
            preferred_element_type=jnp.float32,
        )
        return ((key_total, content_accumulated, table_total + table_part), query_part)

    start_state = (
        jnp.zeros(key_rows.shape, jnp.float32),
        jnp.zeros(value_rows.shape, jnp.float32),
        jnp.zeros(bucket_bias_table.shape, jnp.float32),
    )
    (key_grad, value_grad, table_grad), query_parts = lax.scan(
        step_forward, start_state, jnp.arange(total_rows // block_rows, dtype=jnp.int32)
    )
    return (query_parts.reshape(queries.shape), key_grad, value_grad, table_grad)


def project(normed, weight, head_count):
    projected = jnp.dot(normed, weight, preferred_element_type=jnp.float32).astype(jnp.bfloat16)
    return projected.reshape(normed.shape[0], head_count, DH)


def body(
    inputs,
    segments,
    first_gain,
    query_weight,
    lookup_projection,
    value_weight,
    output_weight,
    bucket_bias_table,
    second_gain,
    inner_weight,
    outer_weight,
    cotangent,
):
    total_rows = segments.shape[0]
    head_count = query_weight.shape[1] // DH
    block_rows = min(512, total_rows)
    gain_one = first_gain.astype(jnp.float32)
    gain_two = second_gain.astype(jnp.float32)
    factor = float(total_rows * lax.axis_size("dp")) ** (-0.5)
    norm_input = inputs.astype(jnp.float32)
    normed_value, inverse_one = root_norm(norm_input, gain_one)
    normed_one = lax.all_gather(normed_value.astype(jnp.bfloat16), "tensor", axis=0, tiled=True)
    queries = project(normed_one, query_weight, head_count)
    key_rows = project(normed_one, lookup_projection, head_count)
    value_rows = project(normed_one, value_weight, head_count)
    context, logsum = attend_forward(
        queries, key_rows, value_rows, segments, bucket_bias_table, block_rows
    )
    attended_part = jnp.dot(context, output_weight, preferred_element_type=jnp.float32)
    middle = norm_input + lax.psum_scatter(attended_part, "tensor", scatter_dimension=0, tiled=True)
    normed_value, inverse_two = root_norm(middle, gain_two)
    normed_two = lax.all_gather(normed_value.astype(jnp.bfloat16), "tensor", axis=0, tiled=True)
    inner_value = jnp.dot(normed_two, inner_weight, preferred_element_type=jnp.float32)
    hidden_value, gate_pullback = jax.vjp(smooth_gate, inner_value)
    hidden = hidden_value.astype(jnp.bfloat16)
    outer_part = jnp.dot(hidden, outer_weight, preferred_element_type=jnp.float32)
    layer_output = (
        middle
        + lax.psum_scatter(
            outer_part.astype(jnp.bfloat16), "tensor", scatter_dimension=0, tiled=True
        ).astype(jnp.float32)
    ).astype(jnp.bfloat16)
    full_cotangent = lax.all_gather(cotangent, "tensor", axis=0, tiled=True)
    hidden_grad = jnp.dot(full_cotangent, outer_weight.T, preferred_element_type=jnp.float32)
    inner_grad = gate_pullback(hidden_grad)[0].astype(jnp.bfloat16)
    outer_weight_grad = jnp.dot(hidden.T, full_cotangent, preferred_element_type=jnp.float32)
    inner_weight_grad = jnp.dot(normed_two.T, inner_grad, preferred_element_type=jnp.float32)
    rescaled_second_share = jnp.dot(inner_grad, inner_weight.T, preferred_element_type=jnp.float32)
    normed_two_grad = lax.psum_scatter(
        rescaled_second_share, "tensor", scatter_dimension=0, tiled=True
    )
    middle_grad = cotangent.astype(jnp.float32) + norm_input_grad(
        middle, inverse_two, gain_two, normed_two_grad
    )
    gain_two_part = norm_gain_grad(middle, inverse_two, normed_two_grad)
    attended_grad = lax.all_gather(middle_grad.astype(jnp.bfloat16), "tensor", axis=0, tiled=True)
    output_weight_grad = jnp.dot(context.T, attended_grad, preferred_element_type=jnp.float32)
    context_grad = jnp.dot(
        attended_grad, output_weight.T, preferred_element_type=jnp.float32
    ).astype(jnp.bfloat16)
    context_grad = context_grad.reshape(total_rows, head_count, DH)
    query_part, key_part, value_part, table_grad = attend_backward(
        queries, key_rows, value_rows, segments, bucket_bias_table, logsum, context_grad, block_rows
    )
    query_grad = query_part.astype(jnp.bfloat16).reshape(total_rows, -1)
    key_grad = key_part.astype(jnp.bfloat16).reshape(total_rows, -1)
    value_grad = value_part.astype(jnp.bfloat16).reshape(total_rows, -1)
    query_weight_grad = jnp.dot(normed_one.T, query_grad, preferred_element_type=jnp.float32)
    key_weight_grad = jnp.dot(normed_one.T, key_grad, preferred_element_type=jnp.float32)
    content_projection_adjoint = jnp.dot(
        normed_one.T, value_grad, preferred_element_type=jnp.float32
    )
    normed_one_part = jnp.dot(query_grad, query_weight.T, preferred_element_type=jnp.float32)
    normed_one_part = normed_one_part + jnp.dot(
        key_grad, lookup_projection.T, preferred_element_type=jnp.float32
    )
    normed_one_part = normed_one_part + jnp.dot(
        value_grad, value_weight.T, preferred_element_type=jnp.float32
    )
    normed_one_grad = lax.psum_scatter(
        normed_one_part.astype(jnp.bfloat16), "tensor", scatter_dimension=0, tiled=True
    ).astype(jnp.float32)
    input_grad = middle_grad + norm_input_grad(norm_input, inverse_one, gain_one, normed_one_grad)
    gain_one_part = norm_gain_grad(norm_input, inverse_one, normed_one_grad)
    gain_grads = lax.psum(jnp.stack([gain_one_part, gain_two_part]), ("dp", "tensor")) * factor
    (
        query_weight_grad,
        key_weight_grad,
        content_projection_adjoint,
        output_weight_grad,
        table_grad,
        inner_weight_grad,
        outer_weight_grad,
    ) = lax.psum(
        (
            query_weight_grad,
            key_weight_grad,
            content_projection_adjoint,
            output_weight_grad,
            table_grad,
            inner_weight_grad,
            outer_weight_grad,
        ),
        "dp",
    )
    return (
        layer_output,
        input_grad,
        query_weight_grad * factor,
        key_weight_grad * factor,
        content_projection_adjoint * factor,
        output_weight_grad * factor,
        table_grad * factor,
        inner_weight_grad * factor,
        outer_weight_grad * factor,
        gain_grads,
    )


def solution(mesh):
    return jax.shard_map(
        body,
        mesh=mesh,
        in_specs=(
            P(("dp", "tensor"), None),
            P("dp"),
            P(),
            P(None, "tensor"),
            P(None, "tensor"),
            P(None, "tensor"),
            P("tensor", None),
            P(None, "tensor"),
            P(),
            P(None, "tensor"),
            P("tensor", None),
            P(("dp", "tensor"), None),
        ),
        out_specs=(
            P(("dp", "tensor"), None),
            P(("dp", "tensor"), None),
            P(None, "tensor"),
            P(None, "tensor"),
            P(None, "tensor"),
            P("tensor", None),
            P(None, "tensor"),
            P(None, "tensor"),
            P("tensor", None),
            P(),
        ),
        check_vma=False,
    )
```

profile of v0, /device:TPU:0, one launch (start us, length us, event | category | flops | bytes accessed | tf_op | source)
XLA Modules:
  0.0 1009.0 jit_solution(12766464865218102238)
XLA Ops:
  12.6 26.8 %all-gather.5.cloned.1.call-done = bf16[1536,768]{1,0:T(8,128)(2,1)} async-done(((bf16[384,768]{1,0:T(8,128)(2,1)}), bf16[1536,768]{1,0:T(8,128)(2,1)}) %all-gather.5.cloned.1.call-update) | async-done | bytes 2359312 | tf_op jit(solution)/shard_map/all_gather | solution.py:165
  39.5 2.7 convolution_convert_fusion.2
  44.1 108.2 %while.29 = (s32[]{:T(128)}, bf16[3,512,3,64]{1,3,2,0:T(8,128)(2,1)}, f32[3,3,512,1]{2,1,3,0:T(4,128)}, s32[3]{0:T(128)S(1)}, s32[1536]{0:T(1024)S(1)}, /*index=...) while((s32[]{:T(128)}, ...), condition=%wide.region_4.5_spmd, body=%wide.region_1.4_spmd.sunk | while | flops 824278016 | bytes 56691088 | solution.py:82
  46.0 3.5 fusion.163
  49.5 16.8 %fusion.164 = f32[512,1536,3]{1,2,0:T(4,128)} fusion(s32[512,1536]{1,0:T(8,128)S(1)} %fusion.163, bf16[32,3]{0,1:T(4,128)(2,1)S(1)} %get-tuple-element.424), kind=kOutput, calls=%fused_computation.1.clone.1 | convolution fusion | flops 176160768 | bytes 12583104 | tf_op jit(solution)/shard_map/while/body/eval_jaxpr/gmn,gi->imn/dot_general | solution.py:57
  66.3 8.8 fusion.165
  76.5 3.0 fusion.167
  82.0 3.5 fusion.163
  85.5 16.8 %fusion.164 = f32[512,1536,3]{1,2,0:T(4,128)} fusion(s32[512,1536]{1,0:T(8,128)S(1)} %fusion.163, bf16[32,3]{0,1:T(4,128)(2,1)S(1)} %get-tuple-element.424), kind=kOutput, calls=%fused_computation.1.clone.1 | convolution fusion | flops 176160768 | bytes 12583104 | tf_op jit(solution)/shard_map/while/body/eval_jaxpr/gmn,gi->imn/dot_general | solution.py:57
  102.3 8.8 fusion.165
  112.5 3.0 fusion.167
  117.9 3.5 fusion.163
  121.4 16.8 %fusion.164 = f32[512,1536,3]{1,2,0:T(4,128)} fusion(s32[512,1536]{1,0:T(8,128)S(1)} %fusion.163, bf16[32,3]{0,1:T(4,128)(2,1)S(1)} %get-tuple-element.424), kind=kOutput, calls=%fused_computation.1.clone.1 | convolution fusion | flops 176160768 | bytes 12583104 | tf_op jit(solution)/shard_map/while/body/eval_jaxpr/gmn,gi->imn/dot_general | solution.py:57
  138.3 8.8 fusion.165
  148.5 3.0 fusion.167
  154.3 4.2 fusion.82
  159.3 47.2 %reduce-scatter.5.cloned.1.call-done = f32[384,768]{1,0:T(8,128)} async-done(((f32[1536,768]{1,0:T(8,128)}), f32[384,768]{1,0:T(8,128)}) %reduce-scatter.5.cloned.1.call-update) | async-done | bytes 1179664 | tf_op jit(solution)/shard_map/reduce_scatter | solution.py:173
  209.8 22.4 %all-gather.9.cloned.1.call-done = bf16[1536,768]{1,0:T(8,128)(2,1)} async-done(((bf16[384,768]{1,0:T(8,128)(2,1)}), bf16[1536,768]{1,0:T(8,128)(2,1)}) %all-gather.9.cloned.1.call-update) | async-done | bytes 2359312 | tf_op jit(solution)/shard_map/all_gather | solution.py:186
  232.3 6.1 fusion.83
  238.4 20.0 %all-gather.7.cloned.1.call-done = bf16[1536,768]{1,0:T(8,128)(2,1)} async-done(((bf16[384,768]{1,0:T(8,128)(2,1)}), bf16[1536,768]{1,0:T(8,128)(2,1)}) %all-gather.7.cloned.1.call-update) | async-done | bytes 2359312 | tf_op jit(solution)/shard_map/all_gather | solution.py:175
  258.4 9.1 fusion.68
  269.0 4.2 fusion.84
  274.5 6.7 convolution_convert_fusion
  281.2 40.0 %reduce-scatter.9.cloned.1.call-done = f32[384,768]{1,0:T(8,128)} async-done(((f32[1536,768]{1,0:T(8,128)}), f32[384,768]{1,0:T(8,128)}) %reduce-scatter.9.cloned.1.call-update) | async-done | bytes 1179664 | tf_op jit(solution)/shard_map/reduce_scatter | solution.py:192
  324.1 33.2 %reduce-scatter.7.cloned.1.call-done = bf16[384,768]{1,0:T(8,128)(2,1)} async-done(((bf16[1536,768]{1,0:T(8,128)(2,1)}), bf16[384,768]{1,0:T(8,128)(2,1)}) %reduce-scatter.7.cloned.1.call-update) | async-done | bytes 589840 | tf_op jit(solution)/shard_map/reduce_scatter | solution.py:182
  357.3 3.1 fusion.80
  360.5 24.1 %all-gather.11.cloned.1.call-done = bf16[1536,768]{1,0:T(8,128)(2,1)} async-done(((bf16[384,768]{1,0:T(8,128)(2,1)}), bf16[1536,768]{1,0:T(8,128)(2,1)}) %all-gather.11.cloned.1.call-update) | async-done | bytes 2359312 | tf_op jit(solution)/shard_map/all_gather | solution.py:199
  384.6 3.4 convolution_convert_fusion.1
  388.5 320.6 %while.30 = (s32[]{:T(128)}, f32[1536,3,64]{0,2,1:T(8,128)}, f32[1536,3,64]{0,2,1:T(8,128)S(1)}, f32[32,3]{0,1:T(4,128)S(1)}, bf16[3,512,3,64]{1,3,2,0:T(8,128)(...) while((s32[]{:T(128)}, f32[1536,3,64]{0,2,1:T(8,128)}, ...), condition=%wide.region_12.13_spmd.clone, body=%wide.region_10.12_spmd.clone.sunk | while | flops 1909849344 | bytes 182304096 | solution.py:132
  405.8 3.4 fusion.180
  409.2 6.2 fusion.179
  415.4 16.8 %fusion.181 = f32[512,1536,3]{0,2,1:T(4,128)} fusion(s32[512,1536]{0,1:T(8,128)S(1)} %fusion.180, bf16[32,3]{0,1:T(4,128)(2,1)S(1)} %get-tuple-element.475), kind=kOutput, calls=%fused_computation.33.clone.1 | convolution fusion | flops 176160768 | bytes 12583104 | tf_op jit(solution)/shard_map/while/body/eval_jaxpr/gmn,gi->imn/dot_general | solution.py:57
  432.2 13.3 %copy.40 = f32[512,1536,3]{1,0,2:T(8,128)} copy(f32[512,1536,3]{0,2,1:T(4,128)} %fusion.181) | data formatting | bytes 18874368 | tf_op jit(solution)/shard_map/while/body/eval_jaxpr/gmn,gi->imn/dot_general | solution.py:57
  445.5 10.4 %multiply_reduce_fusion.5 = (f32[3,512]{1,0:T(4,128)S(1)}, f32[3,512,1536]{2,1,0:T(8,128)}) fusion(f32[3,512,1536]{2,1,0:T(8,128)} %fusion.179, f32[3,512]{1,0:T(4,128)S(1)} %dynamic-slice_bitcast_fusion.2, f32[512,1536,3]{1,0,2:T(8,128)} %copy.40, bf16[1536,3,64]{0,2,1:T(8,128)(2,1)S(1)} %get-tuple-element.474, ...), kind=kOutput, calls=%fused_computation.41.clone.1 | convolution fusion | flops 313784832 | bytes 29896708 | tf_op jit(solution)/shard_map/while/body/eval_jaxpr/qhd,khd->hqk/dot_general | solution.py:49
  455.9 9.5 multiply_convert_fusion.6
  465.4 5.0 fusion.183
  474.7 11.2 %copy.41 = bf16[3,512,1536]{1,0,2:T(4,128)(2,1)} copy(bf16[3,512,1536]{2,1,0:T(8,128)(2,1)} %multiply_convert_fusion.6) | data formatting | bytes 9437184 | tf_op jit(solution)/shard_map/while/body/eval_jaxpr/convert_element_type | solution.py:106
  485.9 17.6 %fusion.184 = f32[32,3]{0,1:T(4,128)S(1)} fusion(bf16[3,512,1536]{1,0,2:T(4,128)(2,1)} %copy.41, s32[512,1536]{0,1:T(8,128)} %copy-done.3, f32[32,3]{0,1:T(4,128)S(1)} %get-tuple-element.451, pred[]{:T(512)S(6)} %compare.3), kind=kOutput, calls=%fused_computation.65.clone.1 | convolution fusion | flops 176160960 | bytes 7865089 | tf_op jit(solution)/shard_map/while/body/eval_jaxpr/swf,kwf->ks/dot_general | solution.py:119
  508.5 3.4 fusion.180
  512.0 6.2 fusion.179
  518.1 16.8 %fusion.181 = f32[512,1536,3]{0,2,1:T(4,128)} fusion(s32[512,1536]{0,1:T(8,128)S(1)} %fusion.180, bf16[32,3]{0,1:T(4,128)(2,1)S(1)} %get-tuple-element.475), kind=kOutput, calls=%fused_computation.33.clone.1 | convolution fusion | flops 176160768 | bytes 12583104 | tf_op jit(solution)/shard_map/while/body/eval_jaxpr/gmn,gi->imn/dot_general | solution.py:57
  534.9 13.3 %copy.40 = f32[512,1536,3]{1,0,2:T(8,128)} copy(f32[512,1536,3]{0,2,1:T(4,128)} %fusion.181) | data formatting | bytes 18874368 | tf_op jit(solution)/shard_map/while/body/eval_jaxpr/gmn,gi->imn/dot_general | solution.py:57
  548.2 10.4 %multiply_reduce_fusion.5 = (f32[3,512]{1,0:T(4,128)S(1)}, f32[3,512,1536]{2,1,0:T(8,128)}) fusion(f32[3,512,1536]{2,1,0:T(8,128)} %fusion.179, f32[3,512]{1,0:T(4,128)S(1)} %dynamic-slice_bitcast_fusion.2, f32[512,1536,3]{1,0,2:T(8,128)} %copy.40, bf16[1536,3,64]{0,2,1:T(8,128)(2,1)S(1)} %get-tuple-element.474, ...), kind=kOutput, calls=%fused_computation.41.clone.1 | convolution fusion | flops 313784832 | bytes 29896708 | tf_op jit(solution)/shard_map/while/body/eval_jaxpr/qhd,khd->hqk/dot_general | solution.py:49
  558.6 9.5 multiply_convert_fusion.6
  568.1 5.0 fusion.183
  577.4 11.2 %copy.41 = bf16[3,512,1536]{1,0,2:T(4,128)(2,1)} copy(bf16[3,512,1536]{2,1,0:T(8,128)(2,1)} %multiply_convert_fusion.6) | data formatting | bytes 9437184 | tf_op jit(solution)/shard_map/while/body/eval_jaxpr/convert_element_type | solution.py:106
  588.6 17.6 %fusion.184 = f32[32,3]{0,1:T(4,128)S(1)} fusion(bf16[3,512,1536]{1,0,2:T(4,128)(2,1)} %copy.41, s32[512,1536]{0,1:T(8,128)} %copy-done.3, f32[32,3]{0,1:T(4,128)S(1)} %get-tuple-element.451, pred[]{:T(512)S(6)} %compare.3), kind=kOutput, calls=%fused_computation.65.clone.1 | convolution fusion | flops 176160960 | bytes 7865089 | tf_op jit(solution)/shard_map/while/body/eval_jaxpr/swf,kwf->ks/dot_general | solution.py:119
  611.2 3.4 fusion.180
  614.7 6.2 fusion.179
  620.8 16.8 %fusion.181 = f32[512,1536,3]{0,2,1:T(4,128)} fusion(s32[512,1536]{0,1:T(8,128)S(1)} %fusion.180, bf16[32,3]{0,1:T(4,128)(2,1)S(1)} %get-tuple-element.475), kind=kOutput, calls=%fused_computation.33.clone.1 | convolution fusion | flops 176160768 | bytes 12583104 | tf_op jit(solution)/shard_map/while/body/eval_jaxpr/gmn,gi->imn/dot_general | solution.py:57
  637.6 13.3 %copy.40 = f32[512,1536,3]{1,0,2:T(8,128)} copy(f32[512,1536,3]{0,2,1:T(4,128)} %fusion.181) | data formatting | bytes 18874368 | tf_op jit(solution)/shard_map/while/body/eval_jaxpr/gmn,gi->imn/dot_general | solution.py:57
  650.9 10.4 %multiply_reduce_fusion.5 = (f32[3,512]{1,0:T(4,128)S(1)}, f32[3,512,1536]{2,1,0:T(8,128)}) fusion(f32[3,512,1536]{2,1,0:T(8,128)} %fusion.179, f32[3,512]{1,0:T(4,128)S(1)} %dynamic-slice_bitcast_fusion.2, f32[512,1536,3]{1,0,2:T(8,128)} %copy.40, bf16[1536,3,64]{0,2,1:T(8,128)(2,1)S(1)} %get-tuple-element.474, ...), kind=kOutput, calls=%fused_computation.41.clone.1 | convolution fusion | flops 313784832 | bytes 29896708 | tf_op jit(solution)/shard_map/while/body/eval_jaxpr/qhd,khd->hqk/dot_general | solution.py:49
  661.3 9.5 multiply_convert_fusion.6
  670.8 5.0 fusion.183
  680.1 11.2 %copy.41 = bf16[3,512,1536]{1,0,2:T(4,128)(2,1)} copy(bf16[3,512,1536]{2,1,0:T(8,128)(2,1)} %multiply_convert_fusion.6) | data formatting | bytes 9437184 | tf_op jit(solution)/shard_map/while/body/eval_jaxpr/convert_element_type | solution.py:106
  691.3 17.6 %fusion.184 = f32[32,3]{0,1:T(4,128)S(1)} fusion(bf16[3,512,1536]{1,0,2:T(4,128)(2,1)} %copy.41, s32[512,1536]{0,1:T(8,128)} %copy-done.3, f32[32,3]{0,1:T(4,128)S(1)} %get-tuple-element.451, pred[]{:T(512)S(6)} %compare.3), kind=kOutput, calls=%fused_computation.65.clone.1 | convolution fusion | flops 176160960 | bytes 7865089 | tf_op jit(solution)/shard_map/while/body/eval_jaxpr/swf,kwf->ks/dot_general | solution.py:119
  715.5 6.0 fusion.88
  721.5 7.0 fusion.79
  735.4 21.2 %psum.60 = f32[32,3]{0,1:T(4,128)S(1)} all-reduce(f32[32,3]{0,1:T(4,128)S(1)} %get-tuple-element.133), channel_id=1, replica_groups=mesh['dp'=8,'tensor'=4] {'dp'}, use_global_device_ids=true, to_apply=%region_19.20 | all-reduce | flops 96 | bytes 768 | tf_op jit(solution)/shard_map/psum | solution.py:237
  758.8 41.6 %psum.63 = f32[2,768]{1,0:T(2,128)S(1)} all-reduce(f32[2,768]{1,0:T(2,128)S(1)} %pad_maximum_fusion), channel_id=1, replica_groups=mesh['dp'=8,'tensor'=4] {'dp','tensor'}, use_global_device_ids=true, to_apply=%region_24.25 | all-reduce | flops 1536 | bytes 12288 | tf_op jit(solution)/shard_map/psum | solution.py:228
  801.0 2.5 fusion.71
  803.5 189.7 %all-reduce.3.cloned.1.call-done = (f32[768,192]{0,1:T(8,128)}, f32[768,192]{0,1:T(8,128)}, f32[768,192]{0,1:T(8,128)}, f32[192,768]{1,0:T(8,128)}, f32[768,768]{1,0:T(8,128)}, /*index=5*/f32[768,768]{1,0:T(8,128)}) async-done(((f32[768,192]{0,1:T(8,128)}, f32[768,192]{0,1:T(8,128)}, f32[768,192]{0,1:T(8,128)}, f32[192,768]{1,0:T(8,128)}, f32[768,768]{1,0:T(8,128)}, /*index=5*/f32[768,768]{1,0:T(8,128)}), ...) | async-done | bytes 7077904 | tf_op jit(solution)/shard_map/psum | solution.py:237
  997.2 2.4 broadcast_multiply_fusion.3
  999.5 2.6 broadcast_multiply_fusion
  (188 shorter events, 69.1 us)
Async XLA Ops:
  7.2 251.3 %copy-start = (bf16[768,768]{1,0:T(8,128)(2,1)S(1)}, bf16[768,768]{1,0:T(8,128)(2,1)}, u32[]{:S(2)}) copy-start(bf16[768,768]{1,0:T(8,128)(2,1)} %param.25) | copy-start | bytes 3538948
  7.2 32.3 %all-gather.5.cloned.1.call-start = ((), (), s32[]{:S(2)}) async-start(), calls=%async_computation.4 | async-start | bytes 2949120 | tf_op jit(solution)/shard_map/all_gather | solution.py:165
  9.1 0.7 copy-start.24
  9.8 0.6 copy-start.22
  12.5 29.7 %copy-start.17 = (bf16[768,192]{0,1:T(8,128)(2,1)S(1)}, bf16[768,192]{0,1:T(8,128)(2,1)}, u32[]{:S(2)}) copy-start(bf16[768,192]{0,1:T(8,128)(2,1)} %param.20) | copy-start | bytes 884740
  12.5 194.0 %reduce-scatter.5.cloned.1.call-start = ((), (), s32[]{:S(2)}) async-start(), calls=%async_computation.5 | async-start | bytes 5898240 | tf_op jit(solution)/shard_map/reduce_scatter | solution.py:173
  39.4 2.8 copy-start.29
  42.2 1.0 copy-start.19
  43.2 0.9 copy-start.16
  43.2 0.9 copy-start.34
  152.3 6.1 copy-start.7
  154.3 4.2 copy-start.9
  158.5 0.8 copy-start.28
  158.5 73.8 %all-gather.9.cloned.1.call-start = ((), (), s32[]{:S(2)}) async-start(), calls=%async_computation.8 | async-start | bytes 2949120 | tf_op jit(solution)/shard_map/all_gather | solution.py:186
  159.2 99.2 %all-gather.7.cloned.1.call-start = ((), (), s32[]{:S(2)}) async-start(), calls=%async_computation.6 | async-start | bytes 2949120 | tf_op jit(solution)/shard_map/all_gather | solution.py:175
  209.8 111.4 %reduce-scatter.9.cloned.1.call-start = ((), (), s32[]{:S(2)}) async-start(), calls=%async_computation.9 | async-start | bytes 5898240 | tf_op jit(solution)/shard_map/reduce_scatter | solution.py:192
  267.6 1.4 copy-start.13
  273.2 1.3 copy-start.33
  273.2 84.0 %reduce-scatter.7.cloned.1.call-start = ((), (), s32[]{:S(2)}) async-start(), calls=%async_computation.7 | async-start | bytes 2949120 | tf_op jit(solution)/shard_map/reduce_scatter | solution.py:182
  281.2 103.5 %all-gather.11.cloned.1.call-start = ((), (), s32[]{:S(2)}) async-start(), calls=%async_computation.10 | async-start | bytes 2949120 | tf_op jit(solution)/shard_map/all_gather | solution.py:199
  321.2 36.1 %copy-start.12 = (f32[384,768]{1,0:T(8,128)S(1)}, f32[384,768]{1,0:T(8,128)}, u32[]{:S(2)}) copy-start(f32[384,768]{1,0:T(8,128)} %reduce-scatter.9.cloned.1.call-done) | copy-start | bytes 3538948
  360.4 28.2 %copy-start.35 = (bf16[32,3]{0,1:T(4,128)(2,1)S(1)}, bf16[32,3]{0,1:T(4,128)(2,1)}, u32[]{:S(2)}) copy-start(bf16[32,3]{0,1:T(4,128)(2,1)} %param.23) | copy-start | bytes 580
  360.4 396.8 %reduce-scatter.11.cloned.1.call-start = ((), (), s32[]{:S(2)}) async-start(), calls=%async_computation.11 | async-start | bytes 2949120 | tf_op jit(solution)/shard_map/reduce_scatter | solution.py:223
  409.2 6.2 copy-start.3
  465.4 5.1 copy-start.2
  470.5 2.2 copy-start.4
  474.7 11.2 %copy-start.5 = (f32[1536,3,64]{0,2,1:T(8,128)}, f32[1536,3,64]{0,2,1:T(8,128)S(1)}, u32[]{:S(2)}) copy-start(f32[1536,3,64]{0,2,1:T(8,128)S(1)} %fusion.182) | copy-start | bytes 3538948 | tf_op jit(solution)/shard_map/while
  511.9 6.2 copy-start.3
  568.1 5.1 copy-start.2
  573.2 2.2 copy-start.4
  577.4 11.2 %copy-start.5 = (f32[1536,3,64]{0,2,1:T(8,128)}, f32[1536,3,64]{0,2,1:T(8,128)S(1)}, u32[]{:S(2)}) copy-start(f32[1536,3,64]{0,2,1:T(8,128)S(1)} %fusion.182) | copy-start | bytes 3538948 | tf_op jit(solution)/shard_map/while
  614.7 6.2 copy-start.3
  670.8 5.1 copy-start.2
  675.9 2.2 copy-start.4
  680.1 11.2 %copy-start.5 = (f32[1536,3,64]{0,2,1:T(8,128)}, f32[1536,3,64]{0,2,1:T(8,128)S(1)}, u32[]{:S(2)}) copy-start(f32[1536,3,64]{0,2,1:T(8,128)S(1)} %fusion.182) | copy-start | bytes 3538948 | tf_op jit(solution)/shard_map/while
  709.2 1.9 copy-start.6
  709.2 2.0 copy-start.18
  711.2 1.0 copy-start.20
  712.2 1.0 copy-start.21
  715.4 277.8 %all-reduce.3.cloned.1.call-start = ((), (), s32[]{:S(2)}) async-start(), calls=%async_computation.12 | async-start | bytes 14155776 | tf_op jit(solution)/shard_map/psum | solution.py:237
  715.4 6.0 copy-start.31
  721.5 7.0 copy-start.10
  721.5 7.0 copy-start.32
  728.5 1.8 copy-start.30
  734.7 0.7 copy-start.26
  734.7 22.5 %copy-start.8 = (bf16[384,768]{1,0:T(8,128)(2,1)S(1)}, bf16[384,768]{1,0:T(8,128)(2,1)}, u32[]{:S(2)}) copy-start(bf16[384,768]{1,0:T(8,128)(2,1)} %param.16) | copy-start | bytes 1769476
  734.7 22.5 %copy-start.23 = (f32[768]{0:T(1024)S(1)}, f32[768]{0:T(1024)}, u32[]{:S(2)}) copy-start(f32[768]{0:T(1024)} %copy-done.22) | copy-start | bytes 9220
  734.7 22.5 %copy-start.25 = (f32[384]{0:T(512)S(1)}, f32[384]{0:T(512)}, u32[]{:S(2)}) copy-start(f32[384]{0:T(512)} %copy-done.24) | copy-start | bytes 4612
  734.7 66.3 %copy-start.11 = (f32[384,768]{1,0:T(8,128)S(1)}, f32[384,768]{1,0:T(8,128)}, u32[]{:S(2)}) copy-start(f32[384,768]{1,0:T(8,128)} %get-tuple-element.231) | copy-start | bytes 3538948
  734.7 66.3 %copy-start.27 = (f32[384]{0:T(512)S(1)}, f32[384]{0:T(512)}, u32[]{:S(2)}) copy-start(f32[384]{0:T(512)} %get-tuple-element.239) | copy-start | bytes 4612
  993.2 6.4 copy-start.14
  993.2 6.4 copy-start.15
  999.5 2.6 copy-start.1
Sparse Core Ops, SparseCore 0:
  12.6 26.7 all-gather.4
  158.6 47.8 reduce-scatter.4
  208.2 24.0 all-gather.8
  234.3 24.0 all-gather.6
  273.3 47.8 reduce-scatter.8
  324.2 33.0 reduce-scatter.6
  360.5 24.0 all-gather.10
  715.5 33.0 reduce-scatter.10
  754.8 238.2 all-reduce.2
where the time goes:
time: 1020 us; the launch traced here: 1010 us
  waiting for transfers between devices  404 us (40%)
  matrix products  327 us (32%)
  local copies, waits for them, and re-layouts  90.8 us (9%)
  other arithmetic  86.5 us (8%)
  blocking collectives  62.8 us (6%)
  loops' own time  22.3 us (2%)
  between operations  14.6 us (1%)
    psum x1, waiting for transfers between devices, body(): lax.psum((query_weight_grad, key_weight_grad, content_projection_adjoint,...  190 us
    dot_general x6, matrix products, score_block(): jnp.einsum('gmn,gi->imn', distance_class_onehot, bucket_bias_table, prefe...  101 us
    dot_general x6, matrix products, score_block(): jnp.einsum('qhd,khd->hqk', query_block, key_rows, preferred_element_type=...  57.7 us
    dot_general x3, matrix products, step_forward(): jnp.einsum('swf,kwf->ks', logit_cotangent, distance_class_onehot, preferr...  52.9 us
    reduce_scatter x1, waiting for transfers between devices, body(): lax.psum_scatter(attended_part, 'tensor', scatter_dimension=0, tiled=True)  47.2 us
    all_gather x2, waiting for transfers between devices, body(): lax.all_gather(normed_value.astype(jnp.bfloat16), 'tensor', axis=0, tiled...  46.9 us
    psum x1, blocking collectives, body(): lax.psum(jnp.stack([gain_one_part, gain_two_part]), ('dp', 'tensor'))  41.6 us
    reduce_scatter x1, waiting for transfers between devices, body(): lax.psum_scatter(rescaled_second_share, 'tensor', scatter_dimension=0, ti...  40 us
  transfers between devices with their start and end apart: 9, of which 8 were waited for; matrix products, arithmetic and copies ran while one was open for 4% of the time, Pallas kernels for 0%

commit v1 on v0

v1 whole, which is shorter than its diff:
```python
import functools

import jax
import jax.numpy as jnp
from jax import lax
from jax.experimental import pallas as pl
from jax.experimental.pallas import tpu as pltpu
from jax.sharding import PartitionSpec as P

DH = 64
LONG = 1024
QT = 256
NEAR = 128
WIDE = 768
EDGES = (8, 12, 16, 23, 32, 46, 64, 91)
EPSILON = 1e-06
MASKED = -1000000000.0
BF = jnp.bfloat16
F32 = jnp.float32


def buckets_of(offset):
    distance = jnp.abs(offset)
    coarse = jnp.full(distance.shape, 7, jnp.int32)
    for boundary in EDGES:
        coarse = coarse + (distance >= boundary).astype(jnp.int32)
    bucket = jnp.where(distance < 8, distance, coarse)
    return bucket + jnp.where(offset > 0, 16, 0).astype(jnp.int32)


def dot(left, right, dims=((1,), (0,))):
    return lax.dot_general(left, right, (dims, ((), ())), preferred_element_type=F32)


ROWS_T = ((1,), (1,))
T_ROWS = ((0,), (0,))


def params(limit=56):
    return pltpu.CompilerParams(vmem_limit_bytes=limit * 1024 * 1024)


def vmem():
    return pl.BlockSpec(memory_space=pltpu.VMEM)


def smem():
    return pl.BlockSpec(memory_space=pltpu.SMEM)


def near_kernel(table_ref, near_ref):
    head_count = near_ref.shape[0]
    lane = lax.broadcasted_iota(jnp.int32, (8, WIDE), 1)
    bucket = buckets_of(lane - (QT + NEAR - 1))
    for head in range(head_count):
        line = jnp.zeros((8, WIDE), F32)
        for slot in range(table_ref.shape[0]):
            line = jnp.where(bucket == slot, table_ref[slot, head], line)
        rows = jnp.broadcast_to(line[:1], (QT, WIDE))
        turned = pltpu.roll(rows, WIDE - QT + 1, 1, stride=1, stride_axis=0)
        near_ref[head] = turned[:, : QT + 2 * NEAR]


def near_bias(table):
    head_count = table.shape[1]
    return pl.pallas_call(
        near_kernel,
        out_shape=jax.ShapeDtypeStruct((head_count, QT, QT + 2 * NEAR), F32),
        in_specs=[smem()],
        out_specs=vmem(),
        compiler_params=params(),
        name="near_bias",
    )(table)


def pieces_of(tile, keys):
    low = max(tile * QT - NEAR, 0)
    high = min(tile * QT + QT + NEAR, keys)
    return low, high, low - (tile * QT - NEAR)


def forward_kernel(
    place_ref,
    table_ref,
    block0,
    block1,
    block2,
    block3,
    weight_ref,
    near_ref,
    row_segment_ref,
    key_segment_ref,
    output_weight_ref,
    query_ref,
    key_ref,
    value_ref,
    prob_ref,
    rest_ref,
    context_ref,
    attended_ref,
    gathered,
):
    head = pl.program_id(0)
    head_count = pl.num_programs(0)
    place = place_ref[0]
    blocks = (block0, block1, block2, block3)
    size = block0.shape[0]
    for step, block in enumerate(blocks):
        row = pl.multiple_of((place ^ step) * size, size)
        made = dot(block[...], weight_ref[0]).astype(BF)
        query_ref[0, pl.ds(row, size), :] = made[:, :DH]
        key_ref[0, pl.ds(row, size), :] = made[:, DH : 2 * DH]
        value_ref[0, pl.ds(row, size), :] = made[:, 2 * DH :]
    total = query_ref.shape[1]
    left_bias = table_ref[15, head]
    right_bias = table_ref[31, head]

    def tiles(first, keys, store_ref, masked):
        for tile in range(keys // QT):
            low, high, lane = pieces_of(tile, keys)
            rows = slice(first + tile * QT, first + tile * QT + QT)
            scores = dot(query_ref[0, rows, :], key_ref[0, first : first + keys, :], ROWS_T)
            parts = []
            if low > 0:
                parts.append((0, low, scores[:, :low] + left_bias))
            parts.append((low, high, scores[:, low:high] + near_ref[0, :, lane : lane + high - low]))
            if high < keys:
                parts.append((high, keys, scores[:, high:] + right_bias))
            if masked:
                row_segment = row_segment_ref[tile * QT : tile * QT + QT, :]
                parts = [
                    (a, b, jnp.where(row_segment == key_segment_ref[:, a:b], part, MASKED))
                    for a, b, part in parts
                ]
            peak = functools.reduce(
                jnp.maximum, [jnp.max(part, axis=1, keepdims=True) for a, b, part in parts]
            )
            parts = [(a, b, jnp.exp(part - peak)) for a, b, part in parts]
            whole = sum(jnp.sum(part, axis=1, keepdims=True) for a, b, part in parts)
            share = 1.0 / whole
            for a, b, part in parts:
                store_ref[0, tile * QT : tile * QT + QT, a:b] = (part * share).astype(BF)
            context_ref[0, rows, :] = dot(
                store_ref[0, tile * QT : tile * QT + QT, :], value_ref[0, first : first + keys, :]
            ).astype(BF)

    tiles(0, LONG, prob_ref, False)
    if total > LONG:
        tiles(LONG, total - LONG, rest_ref, True)
    for which in range(gathered.shape[1] // DH):

        @pl.when(head == which)
        def _():
            gathered[:, which * DH : which * DH + DH] = context_ref[0]

    @pl.when(head == head_count - 1)
    def _():
        for step in range(4):
            row = pl.multiple_of((place ^ step) * size, size)
            attended_ref[step] = dot(
                gathered[pl.ds(row, size), :], output_weight_ref[...]
            ).astype(BF)


def attend_forward(place, table, blocks, weights, near, row_segment, key_segment, output_weight):
    head_count, width, _ = weights.shape
    size = blocks[0].shape[0]
    total = 4 * size
    rest = total - LONG
    by_head = lambda *shape: pl.BlockSpec((1, *shape), lambda h: (h, *(0 for _ in shape)))
    whole = lambda *shape: pl.BlockSpec(shape, lambda h: tuple(0 for _ in shape))
    struct = jax.ShapeDtypeStruct
    return pl.pallas_call(
        forward_kernel,
        grid=(head_count,),
        out_shape=(
            struct((head_count, total, DH), BF),
            struct((head_count, total, DH), BF),
            struct((head_count, total, DH), BF),
            struct((head_count, LONG, LONG), BF),
            struct((head_count, rest, rest), BF),
            struct((head_count, total, DH), BF),
            struct((4, size, width), BF),
        ),
        in_specs=[
            smem(),
            smem(),
            *(whole(size, width) for _ in range(4)),
            by_head(width, 3 * DH),
            by_head(QT, QT + 2 * NEAR),
            whole(rest, 1),
            whole(1, rest),
            whole(head_count * DH, width),
        ],
        out_specs=(
            by_head(total, DH),
            by_head(total, DH),
            by_head(total, DH),
            by_head(LONG, LONG),
            by_head(rest, rest),
            by_head(total, DH),
            whole(4, size, width),
        ),
        scratch_shapes=[pltpu.VMEM((total, head_count * DH), BF)],
        compiler_params=params(),
        cost_estimate=pl.CostEstimate(
            flops=10_000_000_000, bytes_accessed=20_000_000, transcendentals=4_000_000
        ),
        name="attend_forward",
    )(place, table, *blocks, weights, near, row_segment, key_segment, output_weight)


def backward_kernel(
    place_ref,
    grad0,
    grad1,
    grad2,
    grad3,
    block0,
    block1,
    block2,
    block3,
    weight_ref,
    output_weight_ref,
    query_ref,
    key_ref,
    value_ref,
    prob_ref,
    rest_ref,
    context_ref,
    normed_grad_ref,
    weight_grad_ref,
    output_grad_ref,
    line_ref,
    normed_total,
    context_grad,
    near_total,
    far_total,
    parts,
    key_total,
    value_total,
):
    head = pl.program_id(0)
    head_count = pl.num_programs(0)
    place = place_ref[0]
    size = block0.shape[0]
    total = query_ref.shape[1]
    spots = [pl.multiple_of((place ^ step) * size, size) for step in range(4)]
    output_grad = jnp.zeros(output_grad_ref.shape[1:], F32)
    for row, grad in zip(spots, (grad0, grad1, grad2, grad3)):
        context_grad[pl.ds(row, size), :] = dot(grad[...], output_weight_ref[0], ROWS_T).astype(BF)
        output_grad += dot(context_ref[0, pl.ds(row, size), :], grad[...], T_ROWS)
    output_grad_ref[0] = output_grad
    near_total[...] = jnp.zeros_like(near_total)
    far_total[...] = jnp.zeros_like(far_total)

    def tiles(first, keys, stored_ref):
        for tile in range(keys // QT):
            low, high, lane = pieces_of(tile, keys)
            rows = slice(first + tile * QT, first + tile * QT + QT)
            span = slice(first, first + keys)
            local = slice(tile * QT, tile * QT + QT)
            grads = context_grad[rows, :]
            prob = stored_ref[0, local, :]
            prob_grad = dot(grads, value_ref[0, span, :], ROWS_T)
            row_dot = jnp.sum(
                grads.astype(F32) * context_ref[0, rows, :].astype(F32), axis=1, keepdims=True
            )
            score_grad = prob.astype(F32) * (prob_grad - row_dot)
            low_grad = score_grad.astype(BF)
            near_total[:, lane : lane + high - low] += score_grad[:, low:high]
            for side, (a, b) in enumerate(((0, low), (high, keys))):
                if b > a:
                    far_total[side] += sum(
                        score_grad[:, c : c + 128] for c in range(a, b, 128)
                    )
            parts[rows, :DH] = dot(low_grad, key_ref[0, span, :]).astype(BF)
            value_part = dot(grads, prob, T_ROWS)
            key_part = dot(query_ref[0, rows, :], low_grad, T_ROWS)
            if tile == 0:
                value_total[:, span] = value_part
                key_total[:, span] = key_part
            else:
                value_total[:, span] += value_part
                key_total[:, span] += key_part

    tiles(0, LONG, prob_ref)
    if total > LONG:
        tiles(LONG, total - LONG, rest_ref)

    padded = jnp.concatenate(
        [near_total[...], jnp.zeros((QT, WIDE - near_total.shape[1]), F32)], axis=1
    )
    count = QT
    while count > 1:
        count //= 2
        padded = padded[:count] + pltpu.roll(padded[count:], WIDE - count, 1)
    line = pltpu.roll(padded, QT - 1, 1)
    lanes = lax.broadcasted_iota(jnp.int32, line.shape, 1)
    line = jnp.where(lanes == 0, jnp.sum(far_total[0]), line)
    line_ref[0] = jnp.where(lanes == WIDE - 1, jnp.sum(far_total[1]), line)

    key_low = key_total[...].astype(BF)
    value_low = value_total[...].astype(BF)
    parts[:, DH : 2 * DH] = key_total[...].T.astype(BF)
    parts[:, 2 * DH :] = value_total[...].T.astype(BF)
    weight_grad = jnp.zeros(weight_grad_ref.shape[1:], F32)
    for step, (row, block) in enumerate(zip(spots, (block0, block1, block2, block3))):
        taken = parts[pl.ds(row, size), :]
        made = dot(taken, weight_ref[0], ROWS_T)
        weight_grad += dot(taken, block[...], T_ROWS)

        @pl.when(head == 0)
        def _():
            normed_total[step] = made

        @pl.when(head > 0)
        def _():
            normed_total[step] += made

        @pl.when(head == head_count - 1)
        def _():
            normed_grad_ref[step] = normed_total[step].astype(BF)

    weight_grad_ref[0] = weight_grad


def attend_backward(place, grads, blocks, weights, output_weights, kept):
    head_count, width, _ = weights.shape
    size = blocks[0].shape[0]
    total = 4 * size
    rest = total - LONG
    by_head = lambda *shape: pl.BlockSpec((1, *shape), lambda h: (h, *(0 for _ in shape)))
    whole = lambda *shape: pl.BlockSpec(shape, lambda h: tuple(0 for _ in shape))
    struct = jax.ShapeDtypeStruct
    return pl.pallas_call(
        backward_kernel,
        grid=(head_count,),
        out_shape=(
            struct((4, size, width), BF),
            struct((head_count, 3 * DH, width), F32),
            struct((head_count, DH, width), F32),
            struct((head_count, 1, WIDE), F32),
        ),
        in_specs=[
            smem(),
            *(whole(size, width) for _ in range(8)),
            by_head(width, 3 * DH),
            by_head(DH, width),
            by_head(total, DH),
            by_head(total, DH),
            by_head(total, DH),
            by_head(LONG, LONG),
            by_head(rest, rest),
            by_head(total, DH),
        ],
        out_specs=(
            whole(4, size, width),
            by_head(3 * DH, width),
            by_head(DH, width),
            by_head(1, WIDE),
        ),
        scratch_shapes=[
            pltpu.VMEM((4, size, width), F32),
            pltpu.VMEM((total, DH), BF),
            pltpu.VMEM((QT, QT + 2 * NEAR), F32),
            pltpu.VMEM((2, QT, 128), F32),
            pltpu.VMEM((total, 3 * DH), BF),
            pltpu.VMEM((DH, total), F32),
            pltpu.VMEM((DH, total), F32),
        ],
        compiler_params=params(),
        cost_estimate=pl.CostEstimate(
            flops=20_000_000_000, bytes_accessed=20_000_000, transcendentals=0
        ),
        name="attend_backward",
    )(place, *grads, *blocks, weights, output_weights, *kept)


def across(values, axis, flip):
    count = lax.axis_size(axis)
    return lax.ppermute(values, axis, [(i, i ^ flip) for i in range(count)])


def gather_blocks(block):
    far = across(block, "tensor", 2)
    return (block, across(block, "tensor", 1), far, across(far, "tensor", 1))


def scatter_sum(parts):
    sibling = across(jnp.stack([parts[1], parts[3]]), "tensor", 1)
    outward = (parts[2].astype(F32) + sibling[1].astype(F32)).astype(BF)
    far = across(outward, "tensor", 2)
    return parts[0].astype(F32) + sibling[0].astype(F32) + far.astype(F32)


def sum_over_dp(values):
    count = lax.axis_size("dp")
    if count & (count - 1):
        return lax.psum(values, "dp")
    index = lax.axis_index("dp")
    bits = count.bit_length() - 1
    for bit in range(bits):
        half = values.shape[0] // 2
        mine = (index >> bit) & 1
        keep = lax.dynamic_slice_in_dim(values, mine * half, half)
        away = lax.dynamic_slice_in_dim(values, (1 - mine) * half, half)
        came = across(away.astype(BF), "dp", 1 << bit)
        values = keep + came.astype(F32)
    values = values.astype(BF)
    for bit in reversed(range(bits)):
        mine = (index >> bit) & 1
        came = across(values, "dp", 1 << bit)
        first = jnp.where(mine == 0, values, came)
        second = jnp.where(mine == 0, came, values)
        values = jnp.concatenate([first, second])
    return values.astype(F32)


def sum_small(values, axis):
    count = lax.axis_size(axis)
    if count & (count - 1) or count > 8:
        return lax.psum(values, axis)
    return values + sum(across(values, axis, flip) for flip in range(1, count))


def root_norm(values, gains):
    inverse = lax.rsqrt(jnp.mean(values * values, axis=-1, keepdims=True) + EPSILON)
    return (values * inverse * gains, inverse)


def norm_input_grad(values, inverse, gains, upstream):
    scaled = upstream * gains
    projection = jnp.mean(scaled * values, axis=-1, keepdims=True)
    return inverse * scaled - values * (inverse * inverse * inverse) * projection


def norm_gain_grad(values, inverse, upstream):
    return jnp.sum(upstream * values * inverse, axis=0)


def smooth_gate(values):
    return jax.nn.gelu(values, approximate=True)


def body(
    inputs,
    segments,
    first_gain,
    query_weight,
    lookup_projection,
    value_weight,
    output_weight,
    bucket_bias_table,
    second_gain,
    inner_weight,
    outer_weight,
    cotangent,
):
    total = segments.shape[0]
    width = inputs.shape[1]
    head_count = query_weight.shape[1] // DH
    gain_one = first_gain.astype(F32)
    gain_two = second_gain.astype(F32)
    factor = float(total * lax.axis_size("dp")) ** (-0.5)
    place = lax.axis_index("tensor").astype(jnp.int32).reshape(1)
    table = bucket_bias_table.astype(F32)
    heads = lambda weight: weight.reshape(width, head_count, DH).transpose(1, 0, 2)
    weights = jnp.concatenate(
        [heads(query_weight), heads(lookup_projection), heads(value_weight)], axis=2
    )
    near = near_bias(table)
    row_segment = segments[LONG:].reshape(-1, 1)
    key_segment = segments[LONG:].reshape(1, -1)

    norm_input = inputs.astype(F32)
    normed_value, inverse_one = root_norm(norm_input, gain_one)
    normed_one = gather_blocks(normed_value.astype(BF))
    *kept, attended = attend_forward(
        place, table, normed_one, weights, near, row_segment, key_segment, output_weight
    )
    cotangents = gather_blocks(cotangent)
    middle = norm_input + scatter_sum(attended)
    normed_value, inverse_two = root_norm(middle, gain_two)
    normed_two = jnp.concatenate(gather_blocks(normed_value.astype(BF)))
    full_cotangent = jnp.concatenate(cotangents)
    inner_value = dot(normed_two, inner_weight)
    hidden_value, gate_pullback = jax.vjp(smooth_gate, inner_value)
    hidden = hidden_value.astype(BF)
    outer_part = dot(hidden, outer_weight).astype(BF).reshape(4, -1, width)
    hidden_grad = dot(full_cotangent, outer_weight, ROWS_T)
    inner_grad = gate_pullback(hidden_grad)[0].astype(BF)
    second_part = dot(inner_grad, inner_weight, ROWS_T).astype(BF).reshape(4, -1, width)
    outer_weight_grad = dot(hidden, full_cotangent, T_ROWS)
    inner_weight_grad = dot(normed_two, inner_grad, T_ROWS)
    normed_two_grad = scatter_sum(second_part)
    layer_output = (middle + scatter_sum(outer_part)).astype(BF)
    middle_grad = cotangent.astype(F32) + norm_input_grad(
        middle, inverse_two, gain_two, normed_two_grad
    )
    gain_two_part = norm_gain_grad(middle, inverse_two, normed_two_grad)
    attended_grad = gather_blocks(middle_grad.astype(BF))
    normed_one_part, weight_grads, output_weight_grad, line = attend_backward(
        place,
        attended_grad,
        normed_one,
        weights,
        output_weight.reshape(head_count, DH, width),
        kept,
    )
    normed_one_grad = scatter_sum(normed_one_part)
    input_grad = middle_grad + norm_input_grad(norm_input, inverse_one, gain_one, normed_one_grad)
    gain_one_part = norm_gain_grad(norm_input, inverse_one, normed_one_grad)
    gain_grads = jnp.stack([gain_one_part, gain_two_part])
    gain_grads = sum_small(sum_small(gain_grads, "tensor"), "dp")

    slots = jnp.arange(table.shape[0], dtype=jnp.int32)
    offsets = jnp.arange(WIDE, dtype=jnp.int32) - (QT + NEAR - 1)
    chosen = buckets_of(offsets)[None, :] == slots[:, None]
    table_grad = jnp.sum(
        jnp.where(chosen[:, None, :], line.reshape(1, head_count, WIDE), 0.0), axis=2
    )
    table_grad = sum_small(table_grad, "dp")
    outer_weight_grad = sum_over_dp(outer_weight_grad)
    inner_weight_grad = sum_over_dp(inner_weight_grad)
    rows = head_count * DH
    small = jnp.concatenate(
        [weight_grads.reshape(3 * rows, width), output_weight_grad.reshape(rows, width)]
    )
    small = sum_over_dp(small)
    three = small[: 3 * rows].reshape(head_count, 3, DH, width).transpose(1, 3, 0, 2)
    three = three.reshape(3, width, rows)
    return (
        layer_output,
        input_grad,
        three[0] * factor,
        three[1] * factor,
        three[2] * factor,
        small[3 * rows :] * factor,
        table_grad * factor,
        inner_weight_grad * factor,
        outer_weight_grad * factor,
        gain_grads * factor,
    )


def solution(mesh):
    return jax.shard_map(
        body,
        mesh=mesh,
        in_specs=(
            P(("dp", "tensor"), None),
            P("dp"),
            P(),
            P(None, "tensor"),
            P(None, "tensor"),
            P(None, "tensor"),
            P("tensor", None),
            P(None, "tensor"),
            P(),
            P(None, "tensor"),
            P("tensor", None),
            P(("dp", "tensor"), None),
        ),
        out_specs=(
            P(("dp", "tensor"), None),
            P(("dp", "tensor"), None),
            P(None, "tensor"),
            P(None, "tensor"),
            P(None, "tensor"),
            P("tensor", None),
            P(None, "tensor"),
            P(None, "tensor"),
            P("tensor", None),
            P(),
        ),
        check_vma=False,
    )
```

time: 1020 us -> 314 us (0.31)
  matrix products: 327 us -> 18.5 us
  waiting for transfers between devices: 404 us -> 137 us
  local copies, waits for them, and re-layouts: 90.8 us -> 10.4 us
  starting transfers between devices: 0.37 us -> 68.5 us
  other arithmetic: 86.5 us -> 23.7 us
  blocking collectives: 62.8 us -> 0 us
  Pallas kernels: 0 us -> 48.8 us
  loops' own time: 22.3 us -> 0 us
  between operations: 14.6 us -> 1.63 us
    dot_general x48 -> x6, matrix products: 327 us -> 18.5 us  [dot(): lax.dot_general(left, right, (dims, ((), ())), preferred_element_type=F32)]
    psum x1 -> x0, waiting for transfers between devices: 190 us -> none  [body(): lax.psum((query_weight_grad, key_weight_grad, content_projection_adjoint,...]
    ppermute x0 -> x55, waiting for transfers between devices: none -> 137 us  [across(): return lax.ppermute(values, axis, [(i, i ^ flip) for i in range(count)])]
    reduce_scatter x4 -> x0, waiting for transfers between devices: 120 us -> none  [the longest x1 47.2 us: body(): lax.psum_scatter(attended_part, 'tensor', scatter_dimension=0, tiled=True)]
    all_gather x4 -> x0, waiting for transfers between devices: 93.4 us -> none  [the longest x2 46.9 us: body(): lax.all_gather(normed_value.astype(jnp.bfloat16), 'tensor', axis=0, tiled...]
    ppermute x0 -> x55, starting transfers between devices: none -> 68.5 us  [across(): return lax.ppermute(values, axis, [(i, i ^ flip) for i in range(count)])]
    psum x2 -> x0, blocking collectives: 62.8 us -> none  [the longest x1 41.6 us: body(): lax.psum(jnp.stack([gain_one_part, gain_two_part]), ('dp', 'tensor'))]
    pallas_call x0 -> x3, Pallas kernels: none -> 48.8 us  [the longest x1 26.8 us: attend_backward(): pl.pallas_call(backward_kernel, grid=(head_count,), out_shape=(struct((4,...]
  transfers between devices with their start and end apart: 9 -> 55, of which waited for: 8 -> 18; matrix products, arithmetic and copies ran while one was open for 4% -> 9% of each run, Pallas kernels for 0% -> 10%
where the time goes in v1:
time: 314 us; the launch traced here: 308 us
  waiting for transfers between devices  137 us (44%)
  starting transfers between devices  68.5 us (22%)
  Pallas kernels  48.8 us (16%)
  other arithmetic  23.7 us (8%)
  matrix products  18.5 us (6%)
  local copies, waits for them, and re-layouts  10.4 us (3%)
    ppermute x55, waiting for transfers between devices, across(): return lax.ppermute(values, axis, [(i, i ^ flip) for i in range(count)])  137 us
    ppermute x55, starting transfers between devices, across(): return lax.ppermute(values, axis, [(i, i ^ flip) for i in range(count)])  68.5 us
    pallas_call x1, Pallas kernels, attend_backward(): pl.pallas_call(backward_kernel, grid=(head_count,), out_shape=(struct((4,...  26.8 us
    pallas_call x1, Pallas kernels, attend_forward(): pl.pallas_call(forward_kernel, grid=(head_count,), out_shape=(struct((hea...  19.5 us
    dot_general x6, matrix products, dot(): lax.dot_general(left, right, (dims, ((), ())), preferred_element_type=F32)  18.5 us
  transfers between devices with their start and end apart: 55, of which 18 were waited for; matrix products, arithmetic and copies ran while one was open for 9% of the time, Pallas kernels for 10%

profile of v1, /device:TPU:0, one launch (start us, length us, event | category | flops | bytes accessed | tf_op | source)
XLA Modules:
  0.0 308.4 jit_solution(15294421440399262932)
XLA Ops:
  0.7 1.4 fusion.11
  3.3 1.3 fusion.13.block0
  4.7 3.0 collective-permute-start.1
  7.7 13.4 %collective-permute-done.1.block2 = bf16[384,768]{1,0:T(8,128)(2,1)} collective-permute-done((bf16[384,768]{1,0:T(8,128)(2,1)S(1)}, bf16[384,768]{1,0:T(8,128)(2,1)}, u32[]{:S(2)}, u32[]{:S(2)}) %collective-permute-start.1) | collective-permute-done | bytes 589856 | tf_op jit(solution)/shard_map/ppermute | solution.py:382
  24.0 1.3 copy.31
  25.3 2.5 near_bias.1.near_ref
  27.8 1.6 pad_maximum_fusion.1.weight_ref
  29.4 19.5 %attend_forward.1 = (bf16[3,1536,64]{2,1,0:T(8,128)(2,1)}, bf16[3,1536,64]{2,1,0:T(8,128)(2,1)}, bf16[3,1536,64]{2,1,0:T(8,128)(2,1)}, bf16[3,1024,1024]{2,1,0:T...) custom-call(s32[1]{0:T(128)} %bitcast.place_ref, ...), custom_call_target="tpu_custom_call" | custom-call | flops 10000000000 | bytes 20000000 | tf_op jit(solution)/shard_map/attend_forward/pallas_call | solution.py:173
  48.9 1.3 fusion.46
  51.0 2.5 collective-permute-done.3
  53.6 1.8 collective-permute-start.4
  55.7 14.1 %collective-permute-done.4 = bf16[384,768]{1,0:T(8,128)(2,1)S(1)} collective-permute-done((bf16[384,768]{1,0:T(8,128)(2,1)S(1)}, bf16[384,768]{1,0:T(8,128)(2,1)S(1)}, u32[]{:S(2)}, u32[]{:S(2)}) %collective-permute-start.4) | collective-permute-done | bytes 589856 | tf_op jit(solution)/shard_map/ppermute | solution.py:382
  71.8 1.7 collective-permute-start.6
  73.6 9.0 %collective-permute-done.11 = bf16[384,768]{1,0:T(8,128)(2,1)} collective-permute-done((bf16[384,768]{1,0:T(8,128)(2,1)S(1)}, bf16[384,768]{1,0:T(8,128)(2,1)}, u32[]{:S(2)}, u32[]{:S(2)}) %collective-permute-start.11) | collective-permute-done | bytes 589856 | tf_op jit(solution)/shard_map/ppermute | solution.py:382
  83.2 11.5 %collective-permute-done.6 = bf16[384,768]{1,0:T(8,128)(2,1)} collective-permute-done((bf16[384,768]{1,0:T(8,128)(2,1)}, bf16[384,768]{1,0:T(8,128)(2,1)}, u32[]{:S(2)}, u32[]{:S(2)}) %collective-permute-start.6) | collective-permute-done | bytes 589856 | tf_op jit(solution)/shard_map/ppermute | solution.py:382
  95.8 1.2 constant_dynamic-update-slice_fusion.1
  97.2 3.2 %fusion.29 = f32[1536,768]{1,0:T(8,128)S(1)} fusion(bf16[768,768]{1,0:T(8,128)(2,1)S(1)} %copy-done.18, bf16[384,768]{1,0:T(8,128)(2,1)S(1)} %collective-permute-done.7, bf16[384,768]{1,0:T(8,128)(2,1)} %collective-permute-done.6, bf16[384,768]{1,0:T(8,128)(2,1)S(1)} %collective-permute-done.5, bf16[384,768]{1,0:T(8,128)(2,1)} %multiply_convert_fusion.1), kind=kOutput, calls=%fused_computation.97 | convolution fusion | flops 1821376512 | bytes 8257536 | tf_op jit(solution)/shard_map/dot_general | solution.py:32
  100.5 2.9 convolution_convert_fusion.1
  103.4 2.5 fusion.43
  105.9 4.5 %fusion.6 = bf16[1536,768]{1,0:T(8,128)(2,1)S(1)} fusion(f32[1536,768]{1,0:T(8,128)S(1)} %fusion.29, bf16[1536,768]{1,0:T(8,128)(2,1)S(1)} %constant_dynamic-update-slice_fusion, bf16[768,768]{1,0:T(8,128)(2,1)S(1)} %copy-done), kind=kOutput, calls=%fused_computation.8 | convolution fusion | flops 1835532288 | bytes 10616832 | tf_op jit(solution)/shard_map/dot_general | solution.py:32
  111.2 2.0 convolution_convert_fusion
  113.4 1.8 collective-permute-start.39
  115.2 3.3 %fusion.28 = f32[768,768]{1,0:T(8,128)S(1)} fusion(bf16[1536,768]{1,0:T(8,128)(2,1)S(1)} %fusion.6, bf16[384,768]{1,0:T(8,128)(2,1)S(1)} %collective-permute-done.7, bf16[384,768]{1,0:T(8,128)(2,1)} %collective-permute-done.6, bf16[384,768]{1,0:T(8,128)(2,1)S(1)} %collective-permute-done.5, bf16[384,768]{1,0:T(8,128)(2,1)} %multiply_convert_fusion.1), kind=kOutput, calls=%fused_computation.96 | convolution fusion | flops 1821376512 | bytes 7077888 | tf_op jit(solution)/shard_map/dot_general | solution.py:32
  119.2 10.4 %collective-permute-done.39 = bf16[384,768]{1,0:T(8,128)(2,1)S(1)} collective-permute-done((bf16[384,768]{1,0:T(8,128)(2,1)S(1)}, bf16[384,768]{1,0:T(8,128)(2,1)S(1)}, u32[]{:S(2)}, u32[]{:S(2)}) %collective-permute-start.39) | collective-permute-done | bytes 589856 | tf_op jit(solution)/shard_map/ppermute | solution.py:382
  129.8 1.9 collective-permute-start.40
  131.6 9.7 %collective-permute-done.33 = bf16[384,768]{1,0:T(8,128)(2,1)S(1)} collective-permute-done((bf16[384,768]{1,0:T(8,128)(2,1)S(1)}, bf16[384,768]{1,0:T(8,128)(2,1)S(1)}, u32[]{:S(2)}, u32[]{:S(2)}) %collective-permute-start.33) | collective-permute-done | bytes 589856 | tf_op jit(solution)/shard_map/ppermute | solution.py:382
  141.5 1.9 collective-permute-start.34
  143.5 2.7 collective-permute-start.41
  146.1 6.7 %collective-permute-done.34 = bf16[192,768]{1,0:T(8,128)(2,1)S(1)} collective-permute-done((bf16[192,768]{1,0:T(8,128)(2,1)S(1)}, bf16[192,768]{1,0:T(8,128)(2,1)S(1)}, u32[]{:S(2)}, u32[]{:S(2)}) %collective-permute-start.34) | collective-permute-done | bytes 294944 | tf_op jit(solution)/shard_map/ppermute | solution.py:382
  153.1 1.7 collective-permute-start.14
  154.8 1.8 collective-permute-start.35
  158.5 10.9 %collective-permute-done.14 = bf16[384,768]{1,0:T(8,128)(2,1)S(1)} collective-permute-done((bf16[384,768]{1,0:T(8,128)(2,1)S(1)}, bf16[384,768]{1,0:T(8,128)(2,1)S(1)}, u32[]{:S(2)}, u32[]{:S(2)}) %collective-permute-start.14) | collective-permute-done | bytes 589856 | tf_op jit(solution)/shard_map/ppermute | solution.py:382
  169.9 9.4 %collective-permute-done.9 = bf16[384,768]{1,0:T(8,128)(2,1)S(1)} collective-permute-done((bf16[384,768]{1,0:T(8,128)(2,1)S(1)}, bf16[384,768]{1,0:T(8,128)(2,1)S(1)}, u32[]{:S(2)}, u32[]{:S(2)}) %collective-permute-start.9) | collective-permute-done | bytes 589856 | tf_op jit(solution)/shard_map/ppermute | solution.py:382
  179.3 1.5 fusion.44
  180.9 1.6 collective-permute-start.16
  182.5 2.2 collective-permute-start.36
  184.8 2.5 collective-permute-start.43
  187.3 6.1 %collective-permute-done.16.grad2 = bf16[384,768]{1,0:T(8,128)(2,1)S(1)} collective-permute-done((bf16[384,768]{1,0:T(8,128)(2,1)S(1)}, bf16[384,768]{1,0:T(8,128)(2,1)S(1)}, u32[]{:S(2)}, u32[]{:S(2)}) %collective-permute-start.16) | collective-permute-done | bytes 589856 | tf_op jit(solution)/shard_map/ppermute | solution.py:382
  194.3 1.6 collective-permute-start.44
  197.0 26.8 %attend_backward.1 = (bf16[4,384,768]{2,1,0:T(8,128)(2,1)}, f32[3,192,768]{2,1,0:T(8,128)}, f32[3,64,768]{2,1,0:T(8,128)}, f32[3,1,768]{2,1,0:T(1,128)}) custom-call(s32[1]{0:T(128)} %bitcast.place_ref, bf16[384,768]{1,0:T(8,128)(2,1)} %copy-done.8, bf16[384,768]{1,0:T(8,128)(2,1)} %copy-done.20, bf16[384,768]{1,0:T(8,128)(2,1)} %copy-done.19, ...), custom_call_target="tpu_custom_call" | custom-call | flops 20000000000 | bytes 20000000 | tf_op jit(solution)/shard_map/attend_backward/pallas_call | solution.py:336
  223.8 1.5 fusion.8
  227.9 13.8 %collective-permute-done.20 = bf16[384,768]{1,0:T(8,128)(2,1)S(1)} collective-permute-done((bf16[384,768]{1,0:T(8,128)(2,1)S(1)}, bf16[384,768]{1,0:T(8,128)(2,1)S(1)}, u32[]{:S(2)}, u32[]{:S(2)}) %collective-permute-start.20) | collective-permute-done | bytes 589856 | tf_op jit(solution)/shard_map/ppermute | solution.py:382
  242.0 1.5 collective-permute-start.21
  243.8 5.0 %collective-permute-done.21 = bf16[192,768]{1,0:T(8,128)(2,1)S(1)} collective-permute-done((bf16[192,768]{1,0:T(8,128)(2,1)S(1)}, bf16[192,768]{1,0:T(8,128)(2,1)S(1)}, u32[]{:S(2)}, u32[]{:S(2)}) %collective-permute-start.21) | collective-permute-done | bytes 294944 | tf_op jit(solution)/shard_map/ppermute | solution.py:382
  248.9 6.4 %collective-permute-start.22 = (bf16[96,768]{1,0:T(8,128)(2,1)S(1)}, bf16[96,768]{1,0:T(8,128)(2,1)S(1)}, u32[]{:S(2)}, u32[]{:S(2)}) collective-permute-start(bf16[96,768]{1,0:T(8,128)(2,1)S(1)} %dynamic-slice_convert_fusion.7), channel_id=1, source_target_pairs={{0,16},{4,20},{8,24},{12,28},{16,0},{20,4},{24,8},{28,12},{1,17},{... | collective-permute-start | bytes 442376 | tf_op jit(solution)/shard_map/ppermute | solution.py:382
  255.6 6.1 %collective-permute-done.22 = bf16[96,768]{1,0:T(8,128)(2,1)S(1)} collective-permute-done((bf16[96,768]{1,0:T(8,128)(2,1)S(1)}, bf16[96,768]{1,0:T(8,128)(2,1)S(1)}, u32[]{:S(2)}, u32[]{:S(2)}) %collective-permute-start.22) | collective-permute-done | bytes 147488 | tf_op jit(solution)/shard_map/ppermute | solution.py:382
  262.3 1.6 convert_multiply_fusion.6
  264.0 2.1 collective-permute-start.32
  266.1 3.4 %collective-permute-start.30 = (f32[32,3]{0,1:T(4,128)S(1)}, f32[32,3]{0,1:T(4,128)S(1)}, u32[]{:S(2)}, u32[]{:S(2)}) collective-permute-start(f32[32,3]{0,1:T(4,128)S(1)} %select_reduce_fusion), channel_id=1, source_target_pairs={{0,20},{4,16},{8,28},{12,24},{16,4},{20,0},{24,12},{28,8},{1,21},{... | collective-permute-start | bytes 1160 | tf_op jit(solution)/shard_map/ppermute | solution.py:382
  269.4 2.3 collective-permute-start.29
  272.8 2.7 collective-permute-start.26
  275.7 1.5 collective-permute-start.19
  277.1 1.6 convert_multiply_fusion.5
  279.4 2.9 collective-permute-done.24
  282.4 3.1 %collective-permute-done.19 = bf16[384,768]{1,0:T(8,128)(2,1)S(1)} collective-permute-done((bf16[384,768]{1,0:T(8,128)(2,1)S(1)}, bf16[384,768]{1,0:T(8,128)(2,1)S(1)}, u32[]{:S(2)}, u32[]{:S(2)}) %collective-permute-start.19) | collective-permute-done | bytes 589856 | tf_op jit(solution)/shard_map/ppermute | solution.py:382
  286.2 1.6 collective-permute-start.46
  288.1 1.3 collective-permute-start.25
  290.0 2.1 collective-permute-start.54
  292.0 2.5 collective-permute-start.53
  294.5 3.2 %collective-permute-start.51 = (f32[2,768]{1,0:T(2,128)S(1)}, f32[2,768]{1,0:T(2,128)S(1)}, u32[]{:S(2)}, u32[]{:S(2)}) collective-permute-start(f32[2,768]{1,0:T(2,128)S(1)} %add_add_fusion), channel_id=1, source_target_pairs={{0,16},{4,20},{8,24},{12,28},{16,0},{20,4},{24,8},{28,12},{1,17},{... | collective-permute-start | bytes 18440 | tf_op jit(solution)/shard_map/ppermute | solution.py:382
  297.7 2.7 collective-permute-start.49
  301.2 1.5 fusion.16
  302.7 1.5 collective-permute-done.48
  306.2 1.3 slice_multiply_fusion
  (186 shorter events, 26.7 us)
Async XLA Ops:
  0.6 99.9 %copy-start = (bf16[768,768]{1,0:T(8,128)(2,1)S(1)}, bf16[768,768]{1,0:T(8,128)(2,1)}, u32[]{:S(2)}) copy-start(bf16[768,768]{1,0:T(8,128)(2,1)} %param.22) | copy-start | bytes 3538948
  0.7 21.1 %copy-start.17 = (bf16[32,3]{0,1:T(4,128)(2,1)S(1)}, bf16[32,3]{0,1:T(4,128)(2,1)}, u32[]{:S(2)}) copy-start(bf16[32,3]{0,1:T(4,128)(2,1)} %param.19) | copy-start | bytes 580
  0.7 22.7 %copy-start.10 = (bf16[768,192]{0,1:T(8,128)(2,1)S(1)}, bf16[768,192]{0,1:T(8,128)(2,1)}, u32[]{:S(2)}) copy-start(bf16[768,192]{0,1:T(8,128)(2,1)} %param.15) | copy-start | bytes 884740
  3.3 20.4 %copy-start.11 = (bf16[768,192]{0,1:T(8,128)(2,1)S(1)}, bf16[768,192]{0,1:T(8,128)(2,1)}, u32[]{:S(2)}) copy-start(bf16[768,192]{0,1:T(8,128)(2,1)} %param.16) | copy-start | bytes 884740
  4.6 20.7 %copy-start.9 = (bf16[384,768]{1,0:T(8,128)(2,1)}, bf16[384,768]{1,0:T(8,128)(2,1)S(1)}, u32[]{:S(2)}) copy-start(bf16[384,768]{1,0:T(8,128)(2,1)S(1)} %fusion.13.block0) | copy-start | bytes 1769476
  4.7 16.4 %collective-permute-start.1 = (bf16[384,768]{1,0:T(8,128)(2,1)S(1)}, bf16[384,768]{1,0:T(8,128)(2,1)}, u32[]{:S(2)}, u32[]{:S(2)}) collective-permute-start(bf16[384,768]{1,0:T(8,128)(2,1)S(1)} %fusion.13.block0), channel_id=1, source_target_pairs={{0,2},{1,3},{2,0},{3,1},{4,6},{5,7},{6,4},{7,5},{8,10},{9,11},{10,... | collective-permute-start | bytes 1769480 | tf_op jit(solution)/shard_map/ppermute | solution.py:382
  7.7 21.7 %collective-permute-start = (bf16[384,768]{1,0:T(8,128)(2,1)S(1)}, bf16[384,768]{1,0:T(8,128)(2,1)}, u32[]{:S(2)}, u32[]{:S(2)}) collective-permute-start(bf16[384,768]{1,0:T(8,128)(2,1)S(1)} %fusion.13.block0), channel_id=1, source_target_pairs={{0,1},{1,0},{2,3},{3,2},{4,5},{5,4},{6,7},{7,6},{8,9},{9,8},{10,11... | collective-permute-start | bytes 1769480 | tf_op jit(solution)/shard_map/ppermute | solution.py:382
  21.1 8.3 %collective-permute-start.2 = (bf16[384,768]{1,0:T(8,128)(2,1)}, bf16[384,768]{1,0:T(8,128)(2,1)}, u32[]{:S(2)}, u32[]{:S(2)}) collective-permute-start(bf16[384,768]{1,0:T(8,128)(2,1)} %collective-permute-done.1.block2), channel_id=1, source_target_pairs={{0,1},{1,0},{2,3},{3,2},{4,5},{5,4},{6,7},{7,6},{8,9},{9,8},{10,11... | collective-permute-start | bytes 1769480 | tf_op jit(solution)/shard_map/ppermute | solution.py:382
  50.4 19.4 %copy-start.2 = (bf16[384,768]{1,0:T(8,128)(2,1)S(1)}, bf16[384,768]{1,0:T(8,128)(2,1)}, u32[]{:S(2)}) copy-start(bf16[384,768]{1,0:T(8,128)(2,1)} %param.12) | copy-start | bytes 1769476
  50.4 3.0 collective-permute-start.3
  53.6 16.2 %collective-permute-start.4 = (bf16[384,768]{1,0:T(8,128)(2,1)S(1)}, bf16[384,768]{1,0:T(8,128)(2,1)S(1)}, u32[]{:S(2)}, u32[]{:S(2)}) collective-permute-start(bf16[384,768]{1,0:T(8,128)(2,1)S(1)} %fusion.26), channel_id=1, source_target_pairs={{0,2},{1,3},{2,0},{3,1},{4,6},{5,7},{6,4},{7,5},{8,10},{9,11},{10,... | collective-permute-start | bytes 1769480 | tf_op jit(solution)/shard_map/ppermute | solution.py:382
  55.4 27.2 %collective-permute-start.11 = (bf16[384,768]{1,0:T(8,128)(2,1)S(1)}, bf16[384,768]{1,0:T(8,128)(2,1)}, u32[]{:S(2)}, u32[]{:S(2)}) collective-permute-start(bf16[384,768]{1,0:T(8,128)(2,1)S(1)} %copy-done.5), channel_id=1, source_target_pairs={{0,2},{1,3},{2,0},{3,1},{4,6},{5,7},{6,4},{7,5},{8,10},{9,11},{10,... | collective-permute-start | bytes 1769480 | tf_op jit(solution)/shard_map/ppermute | solution.py:382
  71.8 22.8 %collective-permute-start.6 = (bf16[384,768]{1,0:T(8,128)(2,1)}, bf16[384,768]{1,0:T(8,128)(2,1)}, u32[]{:S(2)}, u32[]{:S(2)}) collective-permute-start(bf16[384,768]{1,0:T(8,128)(2,1)} %multiply_convert_fusion.1), channel_id=1, source_target_pairs={{0,2},{1,3},{2,0},{3,1},{4,6},{5,7},{6,4},{7,5},{8,10},{9,11},{10,... | collective-permute-start | bytes 1769480 | tf_op jit(solution)/shard_map/ppermute | solution.py:382
  73.5 21.1 %collective-permute-start.10 = (bf16[384,768]{1,0:T(8,128)(2,1)S(1)}, bf16[384,768]{1,0:T(8,128)(2,1)}, u32[]{:S(2)}, u32[]{:S(2)}) collective-permute-start(bf16[384,768]{1,0:T(8,128)(2,1)S(1)} %copy-done.5), channel_id=1, source_target_pairs={{0,1},{1,0},{2,3},{3,2},{4,5},{5,4},{6,7},{7,6},{8,9},{9,8},{10,11... | collective-permute-start | bytes 1769480 | tf_op jit(solution)/shard_map/ppermute | solution.py:382
  82.6 14.4 %collective-permute-start.12 = (bf16[384,768]{1,0:T(8,128)(2,1)}, bf16[384,768]{1,0:T(8,128)(2,1)S(1)}, u32[]{:S(2)}, u32[]{:S(2)}) collective-permute-start(bf16[384,768]{1,0:T(8,128)(2,1)} %collective-permute-done.11), channel_id=1, source_target_pairs={{0,1},{1,0},{2,3},{3,2},{4,5},{5,4},{6,7},{7,6},{8,9},{9,8},{10,11... | collective-permute-start | bytes 1769480 | tf_op jit(solution)/shard_map/ppermute | solution.py:382
  82.6 14.5 %collective-permute-start.5 = (bf16[384,768]{1,0:T(8,128)(2,1)}, bf16[384,768]{1,0:T(8,128)(2,1)S(1)}, u32[]{:S(2)}, u32[]{:S(2)}) collective-permute-start(bf16[384,768]{1,0:T(8,128)(2,1)} %multiply_convert_fusion.1), channel_id=1, source_target_pairs={{0,1},{1,0},{2,3},{3,2},{4,5},{5,4},{6,7},{7,6},{8,9},{9,8},{10,11... | collective-permute-start | bytes 1769480 | tf_op jit(solution)/shard_map/ppermute | solution.py:382
  94.6 2.4 collective-permute-start.7
  110.7 45.9 %collective-permute-start.8 = (bf16[2,384,768]{2,1,0:T(8,128)(2,1)S(1)}, bf16[2,384,768]{2,1,0:T(8,128)(2,1)S(1)}, u32[]{:S(2)}, u32[]{:S(2)}) collective-permute-start(bf16[2,384,768]{2,1,0:T(8,128)(2,1)S(1)} %pad_maximum_fusion.3), channel_id=1, source_target_pairs={{0,1},{1,0},{2,3},{3,2},{4,5},{5,4},{6,7},{7,6},{8,9},{9,8},{10,11... | collective-permute-start | bytes 3538952 | tf_op jit(solution)/shard_map/ppermute | solution.py:382
  113.4 16.3 %collective-permute-start.39 = (bf16[384,768]{1,0:T(8,128)(2,1)S(1)}, bf16[384,768]{1,0:T(8,128)(2,1)S(1)}, u32[]{:S(2)}, u32[]{:S(2)}) collective-permute-start(bf16[384,768]{1,0:T(8,128)(2,1)S(1)} %dynamic-slice_convert_fusion), channel_id=1, source_target_pairs={{0,4},{4,0},{8,12},{12,8},{16,20},{20,16},{24,28},{28,24},{1,5},{5... | collective-permute-start | bytes 1769480 | tf_op jit(solution)/shard_map/ppermute | solution.py:382
  118.6 22.7 %collective-permute-start.33 = (bf16[384,768]{1,0:T(8,128)(2,1)S(1)}, bf16[384,768]{1,0:T(8,128)(2,1)S(1)}, u32[]{:S(2)}, u32[]{:S(2)}) collective-permute-start(bf16[384,768]{1,0:T(8,128)(2,1)S(1)} %dynamic-slice_convert_fusion.1), channel_id=1, source_target_pairs={{0,4},{4,0},{8,12},{12,8},{16,20},{20,16},{24,28},{28,24},{1,5},{5... | collective-permute-start | bytes 1769480 | tf_op jit(solution)/shard_map/ppermute | solution.py:382
  119.1 33.8 %collective-permute-start.13 = (bf16[2,384,768]{2,1,0:T(8,128)(2,1)S(1)}, bf16[2,384,768]{2,1,0:T(8,128)(2,1)S(1)}, u32[]{:S(2)}, u32[]{:S(2)}) collective-permute-start(bf16[2,384,768]{2,1,0:T(8,128)(2,1)S(1)} %pad_maximum_fusion.4), channel_id=1, source_target_pairs={{0,1},{1,0},{2,3},{3,2},{4,5},{5,4},{6,7},{7,6},{8,9},{9,8},{10,11... | collective-permute-start | bytes 3538952 | tf_op jit(solution)/shard_map/ppermute | solution.py:382
  129.8 13.6 %collective-permute-start.40 = (bf16[192,768]{1,0:T(8,128)(2,1)S(1)}, bf16[192,768]{1,0:T(8,128)(2,1)S(1)}, u32[]{:S(2)}, u32[]{:S(2)}) collective-permute-start(bf16[192,768]{1,0:T(8,128)(2,1)S(1)} %dynamic-slice_convert_fusion.2), channel_id=1, source_target_pairs={{0,8},{4,12},{8,0},{12,4},{16,24},{20,28},{24,16},{28,20},{1,9},{5... | collective-permute-start | bytes 884744 | tf_op jit(solution)/shard_map/ppermute | solution.py:382
  141.5 11.4 %collective-permute-start.34 = (bf16[192,768]{1,0:T(8,128)(2,1)S(1)}, bf16[192,768]{1,0:T(8,128)(2,1)S(1)}, u32[]{:S(2)}, u32[]{:S(2)}) collective-permute-start(bf16[192,768]{1,0:T(8,128)(2,1)S(1)} %dynamic-slice_convert_fusion.3), channel_id=1, source_target_pairs={{0,8},{4,12},{8,0},{12,4},{16,24},{20,28},{24,16},{28,20},{1,9},{5... | collective-permute-start | bytes 884744 | tf_op jit(solution)/shard_map/ppermute | solution.py:382
  143.5 13.9 %collective-permute-start.41 = (bf16[96,768]{1,0:T(8,128)(2,1)S(1)}, bf16[96,768]{1,0:T(8,128)(2,1)S(1)}, u32[]{:S(2)}, u32[]{:S(2)}) collective-permute-start(bf16[96,768]{1,0:T(8,128)(2,1)S(1)} %dynamic-slice_convert_fusion.5), channel_id=1, source_target_pairs={{0,16},{4,20},{8,24},{12,28},{16,0},{20,4},{24,8},{28,12},{1,17},{... | collective-permute-start | bytes 442376 | tf_op jit(solution)/shard_map/ppermute | solution.py:382
  153.1 16.3 %collective-permute-start.14 = (bf16[384,768]{1,0:T(8,128)(2,1)S(1)}, bf16[384,768]{1,0:T(8,128)(2,1)S(1)}, u32[]{:S(2)}, u32[]{:S(2)}) collective-permute-start(bf16[384,768]{1,0:T(8,128)(2,1)S(1)} %fusion.20), channel_id=1, source_target_pairs={{0,2},{1,3},{2,0},{3,1},{4,6},{5,7},{6,4},{7,5},{8,10},{9,11},{10,... | collective-permute-start | bytes 1769480 | tf_op jit(solution)/shard_map/ppermute | solution.py:382
  154.8 27.6 %collective-permute-start.35 = (bf16[96,768]{1,0:T(8,128)(2,1)S(1)}, bf16[96,768]{1,0:T(8,128)(2,1)S(1)}, u32[]{:S(2)}, u32[]{:S(2)}) collective-permute-start(bf16[96,768]{1,0:T(8,128)(2,1)S(1)} %dynamic-slice_convert_fusion.6), channel_id=1, source_target_pairs={{0,16},{4,20},{8,24},{12,28},{16,0},{20,4},{24,8},{28,12},{1,17},{... | collective-permute-start | bytes 442376 | tf_op jit(solution)/shard_map/ppermute | solution.py:382
  156.7 22.6 %collective-permute-start.9 = (bf16[384,768]{1,0:T(8,128)(2,1)S(1)}, bf16[384,768]{1,0:T(8,128)(2,1)S(1)}, u32[]{:S(2)}, u32[]{:S(2)}) collective-permute-start(bf16[384,768]{1,0:T(8,128)(2,1)S(1)} %fusion.22), channel_id=1, source_target_pairs={{0,2},{1,3},{2,0},{3,1},{4,6},{5,7},{6,4},{7,5},{8,10},{9,11},{10,... | collective-permute-start | bytes 1769480 | tf_op jit(solution)/shard_map/ppermute | solution.py:382
  157.4 22.0 %copy-start.14 = (f32[384]{0:T(512)S(1)}, f32[384]{0:T(512)}, u32[]{:S(2)}) copy-start(f32[384]{0:T(512)} %get-tuple-element.72) | copy-start | bytes 4612
  157.4 27.4 %collective-permute-start.42 = (bf16[96,768]{1,0:T(8,128)(2,1)S(1)}, bf16[96,768]{1,0:T(8,128)(2,1)S(1)}, u32[]{:S(2)}, u32[]{:S(2)}) collective-permute-start(bf16[96,768]{1,0:T(8,128)(2,1)S(1)} %add_convert_fusion.2), channel_id=1, source_target_pairs={{0,16},{4,20},{8,24},{12,28},{16,0},{20,4},{24,8},{28,12},{1,17},{... | collective-permute-start | bytes 442376 | tf_op jit(solution)/shard_map/ppermute | solution.py:382
  180.9 12.6 %collective-permute-start.16 = (bf16[384,768]{1,0:T(8,128)(2,1)S(1)}, bf16[384,768]{1,0:T(8,128)(2,1)S(1)}, u32[]{:S(2)}, u32[]{:S(2)}) collective-permute-start(bf16[384,768]{1,0:T(8,128)(2,1)S(1)} %get-tuple-element.36.grad0), channel_id=1, source_target_pairs={{0,2},{1,3},{2,0},{3,1},{4,6},{5,7},{6,4},{7,5},{8,10},{9,11},{10,... | collective-permute-start | bytes 1769480 | tf_op jit(solution)/shard_map/ppermute | solution.py:382
  182.5 11.0 %collective-permute-start.36 = (bf16[96,768]{1,0:T(8,128)(2,1)S(1)}, bf16[96,768]{1,0:T(8,128)(2,1)S(1)}, u32[]{:S(2)}, u32[]{:S(2)}) collective-permute-start(bf16[96,768]{1,0:T(8,128)(2,1)S(1)} %add_convert_fusion.3), channel_id=1, source_target_pairs={{0,16},{4,20},{8,24},{12,28},{16,0},{20,4},{24,8},{28,12},{1,17},{... | collective-permute-start | bytes 442376 | tf_op jit(solution)/shard_map/ppermute | solution.py:382
  184.8 8.8 %collective-permute-start.43 = (bf16[192,768]{1,0:T(8,128)(2,1)S(1)}, bf16[192,768]{1,0:T(8,128)(2,1)S(1)}, u32[]{:S(2)}, u32[]{:S(2)}) collective-permute-start(bf16[192,768]{1,0:T(8,128)(2,1)S(1)} %pad_maximum_fusion.13), channel_id=1, source_target_pairs={{0,8},{4,12},{8,0},{12,4},{16,24},{20,28},{24,16},{28,20},{1,9},{5... | collective-permute-start | bytes 884744 | tf_op jit(solution)/shard_map/ppermute | solution.py:382
  187.3 8.6 %collective-permute-start.15 = (bf16[384,768]{1,0:T(8,128)(2,1)S(1)}, bf16[384,768]{1,0:T(8,128)(2,1)S(1)}, u32[]{:S(2)}, u32[]{:S(2)}) collective-permute-start(bf16[384,768]{1,0:T(8,128)(2,1)S(1)} %get-tuple-element.36.grad0), channel_id=1, source_target_pairs={{0,1},{1,0},{2,3},{3,2},{4,5},{5,4},{6,7},{7,6},{8,9},{9,8},{10,11... | collective-permute-start | bytes 1769480 | tf_op jit(solution)/shard_map/ppermute | solution.py:382
  193.5 2.5 collective-permute-start.17
  193.6 32.8 %collective-permute-start.37 = (bf16[192,768]{1,0:T(8,128)(2,1)S(1)}, bf16[192,768]{1,0:T(8,128)(2,1)S(1)}, u32[]{:S(2)}, u32[]{:S(2)}) collective-permute-start(bf16[192,768]{1,0:T(8,128)(2,1)S(1)} %pad_maximum_fusion.12), channel_id=1, source_target_pairs={{0,8},{4,12},{8,0},{12,4},{16,24},{20,28},{24,16},{28,20},{1,9},{5... | collective-permute-start | bytes 884744 | tf_op jit(solution)/shard_map/ppermute | solution.py:382
  194.3 33.4 %collective-permute-start.44 = (bf16[384,768]{1,0:T(8,128)(2,1)S(1)}, bf16[384,768]{1,0:T(8,128)(2,1)S(1)}, u32[]{:S(2)}, u32[]{:S(2)}) collective-permute-start(bf16[384,768]{1,0:T(8,128)(2,1)S(1)} %pad_maximum_fusion.8), channel_id=1, source_target_pairs={{0,4},{4,0},{8,12},{12,8},{16,20},{20,16},{24,28},{28,24},{1,5},{5... | collective-permute-start | bytes 1769480 | tf_op jit(solution)/shard_map/ppermute | solution.py:382
  225.4 16.3 %collective-permute-start.20 = (bf16[384,768]{1,0:T(8,128)(2,1)S(1)}, bf16[384,768]{1,0:T(8,128)(2,1)S(1)}, u32[]{:S(2)}, u32[]{:S(2)}) collective-permute-start(bf16[384,768]{1,0:T(8,128)(2,1)S(1)} %fusion.8), channel_id=1, source_target_pairs={{0,4},{4,0},{8,12},{12,8},{16,20},{20,16},{24,28},{28,24},{1,5},{5... | collective-permute-start | bytes 1769480 | tf_op jit(solution)/shard_map/ppermute | solution.py:382
  226.5 28.9 %collective-permute-start.38 = (bf16[384,768]{1,0:T(8,128)(2,1)S(1)}, bf16[384,768]{1,0:T(8,128)(2,1)S(1)}, u32[]{:S(2)}, u32[]{:S(2)}) collective-permute-start(bf16[384,768]{1,0:T(8,128)(2,1)S(1)} %pad_maximum_fusion.7), channel_id=1, source_target_pairs={{0,4},{4,0},{8,12},{12,8},{16,20},{20,16},{24,28},{28,24},{1,5},{5... | collective-permute-start | bytes 1769480 | tf_op jit(solution)/shard_map/ppermute | solution.py:382
  227.7 14.0 %copy-start.6 = (f32[3,64,768]{2,1,0:T(8,128)S(1)}, f32[3,64,768]{2,1,0:T(8,128)}, u32[]{:S(2)}) copy-start(f32[3,64,768]{2,1,0:T(8,128)} %get-tuple-element.30) | copy-start | bytes 1769476
  242.0 6.8 %collective-permute-start.21 = (bf16[192,768]{1,0:T(8,128)(2,1)S(1)}, bf16[192,768]{1,0:T(8,128)(2,1)S(1)}, u32[]{:S(2)}, u32[]{:S(2)}) collective-permute-start(bf16[192,768]{1,0:T(8,128)(2,1)S(1)} %dynamic-slice_convert_fusion.4), channel_id=1, source_target_pairs={{0,8},{4,12},{8,0},{12,4},{16,24},{20,28},{24,16},{28,20},{1,9},{5... | collective-permute-start | bytes 884744 | tf_op jit(solution)/shard_map/ppermute | solution.py:382
  243.7 28.0 %collective-permute-start.18 = (bf16[2,384,768]{2,1,0:T(8,128)(2,1)S(1)}, bf16[2,384,768]{2,1,0:T(8,128)(2,1)S(1)}, u32[]{:S(2)}, u32[]{:S(2)}) collective-permute-start(bf16[2,384,768]{2,1,0:T(8,128)(2,1)S(1)} %pad_maximum_fusion.5), channel_id=1, source_target_pairs={{0,1},{1,0},{2,3},{3,2},{4,5},{5,4},{6,7},{7,6},{8,9},{9,8},{10,11... | collective-permute-start | bytes 3538952 | tf_op jit(solution)/shard_map/ppermute | solution.py:382
  248.9 12.8 %collective-permute-start.22 = (bf16[96,768]{1,0:T(8,128)(2,1)S(1)}, bf16[96,768]{1,0:T(8,128)(2,1)S(1)}, u32[]{:S(2)}, u32[]{:S(2)}) collective-permute-start(bf16[96,768]{1,0:T(8,128)(2,1)S(1)} %dynamic-slice_convert_fusion.7), channel_id=1, source_target_pairs={{0,16},{4,20},{8,24},{12,28},{16,0},{20,4},{24,8},{28,12},{1,17},{... | collective-permute-start | bytes 442376 | tf_op jit(solution)/shard_map/ppermute | solution.py:382
  261.7 7.7 %collective-permute-start.23 = (bf16[96,768]{1,0:T(8,128)(2,1)S(1)}, bf16[96,768]{1,0:T(8,128)(2,1)S(1)}, u32[]{:S(2)}, u32[]{:S(2)}) collective-permute-start(bf16[96,768]{1,0:T(8,128)(2,1)S(1)} %add_convert_fusion.4), channel_id=1, source_target_pairs={{0,16},{4,20},{8,24},{12,28},{16,0},{20,4},{24,8},{28,12},{1,17},{... | collective-permute-start | bytes 442376 | tf_op jit(solution)/shard_map/ppermute | solution.py:382
  264.0 8.7 %collective-permute-start.32 = (f32[32,3]{0,1:T(4,128)S(1)}, f32[32,3]{0,1:T(4,128)S(1)}, u32[]{:S(2)}, u32[]{:S(2)}) collective-permute-start(f32[32,3]{0,1:T(4,128)S(1)} %select_reduce_fusion), channel_id=1, source_target_pairs={{0,28},{4,24},{8,20},{12,16},{16,12},{20,8},{24,4},{28,0},{1,29},{... | collective-permute-start | bytes 1160 | tf_op jit(solution)/shard_map/ppermute | solution.py:382
  266.1 6.8 %collective-permute-start.31 = (f32[32,3]{0,1:T(4,128)S(1)}, f32[32,3]{0,1:T(4,128)S(1)}, u32[]{:S(2)}, u32[]{:S(2)}) collective-permute-start(f32[32,3]{0,1:T(4,128)S(1)} %select_reduce_fusion), channel_id=1, source_target_pairs={{0,24},{4,28},{8,16},{12,20},{16,8},{20,12},{24,0},{28,4},{1,25},{... | collective-permute-start | bytes 1160 | tf_op jit(solution)/shard_map/ppermute | solution.py:382
  266.1 9.5 %collective-permute-start.30 = (f32[32,3]{0,1:T(4,128)S(1)}, f32[32,3]{0,1:T(4,128)S(1)}, u32[]{:S(2)}, u32[]{:S(2)}) collective-permute-start(f32[32,3]{0,1:T(4,128)S(1)} %select_reduce_fusion), channel_id=1, source_target_pairs={{0,20},{4,16},{8,28},{12,24},{16,4},{20,0},{24,12},{28,8},{1,21},{... | collective-permute-start | bytes 1160 | tf_op jit(solution)/shard_map/ppermute | solution.py:382
  269.4 6.2 %collective-permute-start.29 = (f32[32,3]{0,1:T(4,128)S(1)}, f32[32,3]{0,1:T(4,128)S(1)}, u32[]{:S(2)}, u32[]{:S(2)}) collective-permute-start(f32[32,3]{0,1:T(4,128)S(1)} %select_reduce_fusion), channel_id=1, source_target_pairs={{0,16},{4,20},{8,24},{12,28},{16,0},{20,4},{24,8},{28,12},{1,17},{... | collective-permute-start | bytes 1160 | tf_op jit(solution)/shard_map/ppermute | solution.py:382
  271.7 7.0 %collective-permute-start.28 = (f32[32,3]{0,1:T(4,128)S(1)}, f32[32,3]{0,1:T(4,128)S(1)}, u32[]{:S(2)}, u32[]{:S(2)}) collective-permute-start(f32[32,3]{0,1:T(4,128)S(1)} %select_reduce_fusion), channel_id=1, source_target_pairs={{0,12},{4,8},{8,4},{12,0},{16,28},{20,24},{24,20},{28,16},{1,13},{... | collective-permute-start | bytes 1160 | tf_op jit(solution)/shard_map/ppermute | solution.py:382
  272.7 6.0 %collective-permute-start.27 = (f32[32,3]{0,1:T(4,128)S(1)}, f32[32,3]{0,1:T(4,128)S(1)}, u32[]{:S(2)}, u32[]{:S(2)}) collective-permute-start(f32[32,3]{0,1:T(4,128)S(1)} %select_reduce_fusion), channel_id=1, source_target_pairs={{0,8},{4,12},{8,0},{12,4},{16,24},{20,28},{24,16},{28,20},{1,9},{5... | collective-permute-start | bytes 1160 | tf_op jit(solution)/shard_map/ppermute | solution.py:382
  272.8 5.9 %collective-permute-start.26 = (f32[32,3]{0,1:T(4,128)S(1)}, f32[32,3]{0,1:T(4,128)S(1)}, u32[]{:S(2)}, u32[]{:S(2)}) collective-permute-start(f32[32,3]{0,1:T(4,128)S(1)} %select_reduce_fusion), channel_id=1, source_target_pairs={{0,4},{4,0},{8,12},{12,8},{16,20},{20,16},{24,28},{28,24},{1,5},{5... | collective-permute-start | bytes 1160 | tf_op jit(solution)/shard_map/ppermute | solution.py:382
  275.6 6.7 %collective-permute-start.24 = (bf16[192,768]{1,0:T(8,128)(2,1)S(1)}, bf16[192,768]{1,0:T(8,128)(2,1)S(1)}, u32[]{:S(2)}, u32[]{:S(2)}) collective-permute-start(bf16[192,768]{1,0:T(8,128)(2,1)S(1)} %pad_maximum_fusion.11), channel_id=1, source_target_pairs={{0,8},{4,12},{8,0},{12,4},{16,24},{20,28},{24,16},{28,20},{1,9},{5... | collective-permute-start | bytes 884744 | tf_op jit(solution)/shard_map/ppermute | solution.py:382
  275.7 9.9 %collective-permute-start.19 = (bf16[384,768]{1,0:T(8,128)(2,1)S(1)}, bf16[384,768]{1,0:T(8,128)(2,1)S(1)}, u32[]{:S(2)}, u32[]{:S(2)}) collective-permute-start(bf16[384,768]{1,0:T(8,128)(2,1)S(1)} %fusion.27), channel_id=1, source_target_pairs={{0,2},{1,3},{2,0},{3,1},{4,6},{5,7},{6,4},{7,5},{8,10},{9,11},{10,... | collective-permute-start | bytes 1769480 | tf_op jit(solution)/shard_map/ppermute | solution.py:382
  286.1 15.1 %copy-start.13 = (f32[384]{0:T(512)S(1)}, f32[384]{0:T(512)}, u32[]{:S(2)}) copy-start(f32[384]{0:T(512)} %get-tuple-element.70) | copy-start | bytes 4612
  286.2 3.3 %collective-permute-start.47 = (f32[2,768]{1,0:T(2,128)S(1)}, f32[2,768]{1,0:T(2,128)S(1)}, u32[]{:S(2)}, u32[]{:S(2)}) collective-permute-start(f32[2,768]{1,0:T(2,128)S(1)} %pad_maximum_fusion.14), channel_id=1, source_target_pairs={{0,3},{1,2},{2,1},{3,0},{4,7},{5,6},{6,5},{7,4},{8,11},{9,10},{10,... | collective-permute-start | bytes 18440 | tf_op jit(solution)/shard_map/ppermute | solution.py:382
  286.2 3.7 %collective-permute-start.46 = (f32[2,768]{1,0:T(2,128)S(1)}, f32[2,768]{1,0:T(2,128)S(1)}, u32[]{:S(2)}, u32[]{:S(2)}) collective-permute-start(f32[2,768]{1,0:T(2,128)S(1)} %pad_maximum_fusion.14), channel_id=1, source_target_pairs={{0,2},{1,3},{2,0},{3,1},{4,6},{5,7},{6,4},{7,5},{8,10},{9,11},{10,... | collective-permute-start | bytes 18440 | tf_op jit(solution)/shard_map/ppermute | solution.py:382
  287.8 2.1 collective-permute-start.45
  288.1 16.7 %collective-permute-start.25 = (bf16[384,768]{1,0:T(8,128)(2,1)S(1)}, bf16[384,768]{1,0:T(8,128)(2,1)S(1)}, u32[]{:S(2)}, u32[]{:S(2)}) collective-permute-start(bf16[384,768]{1,0:T(8,128)(2,1)S(1)} %pad_maximum_fusion.6), channel_id=1, source_target_pairs={{0,4},{4,0},{8,12},{12,8},{16,20},{20,16},{24,28},{28,24},{1,5},{5... | collective-permute-start | bytes 1769480 | tf_op jit(solution)/shard_map/ppermute | solution.py:382
  290.0 7.7 %collective-permute-start.54 = (f32[2,768]{1,0:T(2,128)S(1)}, f32[2,768]{1,0:T(2,128)S(1)}, u32[]{:S(2)}, u32[]{:S(2)}) collective-permute-start(f32[2,768]{1,0:T(2,128)S(1)} %add_add_fusion), channel_id=1, source_target_pairs={{0,28},{4,24},{8,20},{12,16},{16,12},{20,8},{24,4},{28,0},{1,29},{... | collective-permute-start | bytes 18440 | tf_op jit(solution)/shard_map/ppermute | solution.py:382
  292.0 5.7 %collective-permute-start.53 = (f32[2,768]{1,0:T(2,128)S(1)}, f32[2,768]{1,0:T(2,128)S(1)}, u32[]{:S(2)}, u32[]{:S(2)}) collective-permute-start(f32[2,768]{1,0:T(2,128)S(1)} %add_add_fusion), channel_id=1, source_target_pairs={{0,24},{4,28},{8,16},{12,20},{16,8},{20,12},{24,0},{28,4},{1,25},{... | collective-permute-start | bytes 18440 | tf_op jit(solution)/shard_map/ppermute | solution.py:382
  294.5 5.9 %collective-permute-start.52 = (f32[2,768]{1,0:T(2,128)S(1)}, f32[2,768]{1,0:T(2,128)S(1)}, u32[]{:S(2)}, u32[]{:S(2)}) collective-permute-start(f32[2,768]{1,0:T(2,128)S(1)} %add_add_fusion), channel_id=1, source_target_pairs={{0,20},{4,16},{8,28},{12,24},{16,4},{20,0},{24,12},{28,8},{1,21},{... | collective-permute-start | bytes 18440 | tf_op jit(solution)/shard_map/ppermute | solution.py:382
  294.5 8.2 %collective-permute-start.51 = (f32[2,768]{1,0:T(2,128)S(1)}, f32[2,768]{1,0:T(2,128)S(1)}, u32[]{:S(2)}, u32[]{:S(2)}) collective-permute-start(f32[2,768]{1,0:T(2,128)S(1)} %add_add_fusion), channel_id=1, source_target_pairs={{0,16},{4,20},{8,24},{12,28},{16,0},{20,4},{24,8},{28,12},{1,17},{... | collective-permute-start | bytes 18440 | tf_op jit(solution)/shard_map/ppermute | solution.py:382
  297.7 5.0 %collective-permute-start.50 = (f32[2,768]{1,0:T(2,128)S(1)}, f32[2,768]{1,0:T(2,128)S(1)}, u32[]{:S(2)}, u32[]{:S(2)}) collective-permute-start(f32[2,768]{1,0:T(2,128)S(1)} %add_add_fusion), channel_id=1, source_target_pairs={{0,12},{4,8},{8,4},{12,0},{16,28},{20,24},{24,20},{28,16},{1,13},{... | collective-permute-start | bytes 18440 | tf_op jit(solution)/shard_map/ppermute | solution.py:382
  297.7 5.0 %collective-permute-start.49 = (f32[2,768]{1,0:T(2,128)S(1)}, f32[2,768]{1,0:T(2,128)S(1)}, u32[]{:S(2)}, u32[]{:S(2)}) collective-permute-start(f32[2,768]{1,0:T(2,128)S(1)} %add_add_fusion), channel_id=1, source_target_pairs={{0,8},{4,12},{8,0},{12,4},{16,24},{20,28},{24,16},{28,20},{1,9},{5... | collective-permute-start | bytes 18440 | tf_op jit(solution)/shard_map/ppermute | solution.py:382
  300.4 3.8 %collective-permute-start.48 = (f32[2,768]{1,0:T(2,128)S(1)}, f32[2,768]{1,0:T(2,128)S(1)}, u32[]{:S(2)}, u32[]{:S(2)}) collective-permute-start(f32[2,768]{1,0:T(2,128)S(1)} %add_add_fusion), channel_id=1, source_target_pairs={{0,4},{4,0},{8,12},{12,8},{16,20},{20,16},{24,28},{28,24},{1,5},{5... | collective-permute-start | bytes 18440 | tf_op jit(solution)/shard_map/ppermute | solution.py:382
  (13 other events, 53.3 us)
